TPU v7x, 512 devices: a whole 4x8x8 slice. The times are simulated.
512 devices in a mesh: row: 32 (over y_hi, x, core), col: 16 (over y_lo, z).
Axes of the slice: x: 4, y: 8 (y_hi: 4, y_lo: 2; y = y_hi * 2 + y_lo), z: 8, core: 2. Of those that a mesh axis runs over, the one named last changes fastest.
Arguments:
- node_inputs: bfloat16 [65536, 128], P(('col', 'row')), may hold values from -6 to 6
- weight: bfloat16 [128, 256], replicated, may hold values from -0.5 to 0.5
- bias: float32 [256], replicated, may hold values from -2 to 2
- edge_tiles: bfloat16 [32, 1408, 128, 128], P('row', 'col'), may hold values from 0 to 1, as said below
- block_coords: int32 [32, 1408, 2], P('row', 'col'), may hold values from 0 to 31, as said below
- block_counts: int32 [32, 16], P('row', 'col'), may hold values from 1 to 88, as said below
- out_cotangent: bfloat16 [65536, 256], P(('row', 'col')), may hold values from -6 to 6
Outputs:
- activations: bfloat16 [65536, 256], P(('row', 'col'))
- grad_inputs: bfloat16 [65536, 128], P(('col', 'row'))
- grad_weight: float32 [128, 256], replicated
- grad_bias: float32 [256], replicated
Inputs may be any that keep to these rules, and one draw needn't show every extreme that they name: `edge_tiles`: each entry is 0 or 1. `block_coords`: within one grid position the 88 slots name distinct blocks; entry 0 is a block row below 16, entry 1 a block column below 32. Slots at or after the position's count are not part of A. `block_counts`: some grid position has all 88 slots live.
All inputs are finite; a program needn't handle non-finite values.
Results may differ from a plain program's by a relative error of at most 0.025.
Values may be sent and summed in bfloat16 or wider, within the bound.
No kernel may reach another device: no remote copies, remote signals or barrier semaphores. Data moves between devices by JAX's collectives and lax.ppermute only.
A program may use at most 64 MiB of HBM per device.

v0:
```python
import jax
import jax.numpy as jnp
from jax import lax
from jax.sharding import PartitionSpec as P


def group_size_for(slot_total):
    return max((divisor for divisor in range(1, 17) if slot_total % divisor == 0))


def spread_blocks(running, tile_stack, slot_coords, upper_slot, features, transpose):
    group_size = group_size_for(tile_stack.shape[0])
    block_size = tile_stack.shape[1]
    feature_blocks = features.reshape(-1, block_size, features.shape[1])
    source_column = 0 if transpose else 1
    target_column = 1 if transpose else 0
    einsum_form = "sab,saf->sbf" if transpose else "sab,sbf->saf"

    def one_group(group_index, running):
        group_start = group_index * group_size
        tile_group = lax.dynamic_slice_in_dim(tile_stack, group_start, group_size, 0)
        coord_group = lax.dynamic_slice_in_dim(slot_coords, group_start, group_size, 0)
        slot_ids = group_start + jnp.arange(group_size, dtype=jnp.int32)
        live_mask = (slot_ids < upper_slot).astype(tile_group.dtype)
        selected = jnp.take(feature_blocks, coord_group[:, source_column], axis=0)
        product = jnp.einsum(
            einsum_form,
            tile_group * live_mask[:, None, None],
            selected,
            preferred_element_type=jnp.float32,
        )
        return running.at[coord_group[:, target_column]].add(product)

    end_group = (upper_slot + group_size - 1) // group_size
    return lax.fori_loop(0, end_group, one_group, running)


def activate(preactivation, cotangent):
    sigmoid_values = jax.nn.sigmoid(preactivation)
    result = (preactivation * sigmoid_values).astype(jnp.bfloat16)
    gradient = (
        cotangent.astype(jnp.float32)
        * sigmoid_values
        * (1.0 + preactivation * (1.0 - sigmoid_values))
    )
    return (result, gradient)


def per_device(node_inputs, weight, bias, edge_tiles, block_coords, block_counts, out_cotangent):
    piece_rows = node_inputs.shape[0]
    row_devices = lax.axis_size("row")
    col_devices = lax.axis_size("col")
    rows_dev = piece_rows * col_devices
    cols_dev = piece_rows * row_devices
    tile_stack = edge_tiles[0]
    slot_coords = block_coords[0]
    own_count = block_counts[0, 0]
    slot_total = tile_stack.shape[0]
    block_size = tile_stack.shape[1]
    row_blocks = rows_dev // block_size
    col_blocks = cols_dev // block_size
    row_ratio = row_devices // col_devices
    row_index = lax.axis_index("row")
    col_index = lax.axis_index("col")
    diagonal = col_index == row_index // row_ratio
    offset_rows = row_index % row_ratio * rows_dev
    live_all = (jnp.arange(slot_total, dtype=jnp.int32) < own_count).astype(jnp.float32)
    row_counts = jnp.sum(tile_stack, axis=2, dtype=jnp.float32) * live_all[:, None]
    col_counts = jnp.sum(tile_stack, axis=1, dtype=jnp.float32) * live_all[:, None]
    row_part = (
        jnp.zeros((row_blocks, block_size), jnp.float32).at[slot_coords[:, 0]].add(row_counts)
    )
    col_part = (
        jnp.zeros((col_blocks, block_size), jnp.float32).at[slot_coords[:, 1]].add(col_counts)
    )
    col_degree = lax.psum_scatter(
        col_part.reshape(cols_dev), "row", scatter_dimension=0, tiled=True
    )
    row_degree = lax.psum_scatter(
        row_part.reshape(rows_dev), "col", scatter_dimension=0, tiled=True
    )
    col_scale = lax.rsqrt(1.0 + col_degree)[:, None]
    row_scale = lax.rsqrt(1.0 + row_degree)[:, None]
    hidden = (jnp.dot(node_inputs, weight, preferred_element_type=jnp.float32) * col_scale).astype(
        jnp.bfloat16
    )
    gathered = lax.all_gather(hidden, "row", axis=0, tiled=True)
    width = gathered.shape[1]
    running = jnp.zeros((row_blocks, block_size, width), jnp.float32)
    running = spread_blocks(running, tile_stack, slot_coords, own_count, gathered, False)
    running = running.reshape(rows_dev, width)
    own_rows = lax.dynamic_slice_in_dim(gathered, offset_rows, rows_dev, 0).astype(jnp.float32)
    summed = lax.psum_scatter(
        (running + jnp.where(diagonal, own_rows, 0.0)).astype(jnp.bfloat16),
        "col",
        scatter_dimension=0,
        tiled=True,
    ).astype(jnp.float32)
    preactivation = row_scale * summed + bias
    activations, grad_pre = activate(preactivation, out_cotangent)
    cotangent_rows = lax.all_gather(
        (row_scale * grad_pre).astype(jnp.bfloat16), "col", axis=0, tiled=True
    )
    width = cotangent_rows.shape[1]
    running = jnp.zeros((col_blocks, block_size, width), jnp.float32)
    running = spread_blocks(running, tile_stack, slot_coords, own_count, cotangent_rows, True)
    running = running.reshape(cols_dev, width)
    self_term = lax.dynamic_update_slice_in_dim(
        jnp.zeros((cols_dev, width), jnp.float32),
        cotangent_rows.astype(jnp.float32),
        offset_rows,
        0,
    )
    summed_back = lax.psum_scatter(
        (running + jnp.where(diagonal, self_term, 0.0)).astype(jnp.bfloat16),
        "row",
        scatter_dimension=0,
        tiled=True,
    ).astype(jnp.float32)
    grad_hidden = (col_scale * summed_back).astype(jnp.bfloat16)
    weight_part = lax.dot_general(
        node_inputs, grad_hidden, (((0,), (0,)), ((), ())), preferred_element_type=jnp.float32
    )
    grad_inputs = lax.dot_general(
        grad_hidden, weight, (((1,), (1,)), ((), ())), preferred_element_type=jnp.float32
    ).astype(jnp.bfloat16)
    grad_weight, grad_bias = lax.psum((weight_part, jnp.sum(grad_pre, axis=0)), ("row", "col"))
    return (activations, grad_inputs, grad_weight, grad_bias)


def solution(mesh):
    in_specs = (
        P(("col", "row"), None),
        P(),
        P(),
        P("row", "col", None, None),
        P("row", "col", None),
        P("row", "col"),
        P(("row", "col"), None),
    )
    out_specs = (P(("row", "col"), None), P(("col", "row"), None), P(), P())
    return jax.shard_map(
        per_device, mesh=mesh, in_specs=in_specs, out_specs=out_specs, check_vma=False
    )
```

profile of v0, /device:TPU:1, one launch (start us, length us, event | category | flops | bytes accessed | tf_op | source)
XLA Modules:
  0.0 868.7 jit_solution(2562348390320547053)
XLA Ops:
  7.9 0.8 fusion.32
  8.7 3.4 copy.14
  12.1 0.9 convert_reduce_fusion.1
  12.9 1.0 scatter_custom_fusion.3
  13.9 139.0 %all-reduce.1 = f32[4096]{0:T(1024)S(1)} all-reduce(f32[4096]{0:T(1024)S(1)} %bitcast.58), channel_id=3, replica_groups=mesh['row'=32,'col'=16] {'row'}, use_global_device_ids=true, to_apply=%region_5.6.clone | all-reduce | flops 4096 | bytes 32768
  152.9 1.3 dynamic-slice.5
  154.8 0.1 fusion.34
  154.9 0.8 fusion.23
  155.8 64.4 %all-gather.3.cloned.1.call-done = bf16[4096,256]{1,0:T(8,128)(2,1)} async-done(((bf16[128,256]{1,0:T(8,128)(2,1)}), bf16[4096,256]{1,0:T(8,128)(2,1)}) %all-gather.3.cloned.1.call-update) | async-done | bytes 2097168 | tf_op jit(solution)/shard_map/all_gather | solution.py:87
  220.1 1.5 broadcast_in_dim.51
  221.6 16.5 %while.20 = (s32[]{:T(128)}, f32[16,128,256]{2,1,0:T(8,128)}, s32[]{:T(128)}, s32[88,2]{0,1:T(2,128)S(1)}, bf16[88,128,128]{2,1,0:T(8,128)(2,1)}, /*index=5*/s32...) while((s32[]{:T(128)}, f32[16,128,256]{2,1,0:T(8,128)}, ...), condition=%wide.region_8.9_spmd, body=%wide.region_6.8_spmd.sunk | while | flops 93177000 | bytes 8295165 | solution.py:35
  221.6 0.7 compare_convert_fusion.5
  222.3 0.1 constant_dynamic-slice_fusion.4
  222.4 2.2 gather_fusion
  224.6 1.4 fusion.52
  226.0 3.8 scatter_fusion
  229.8 0.6 compare_convert_fusion.5
  230.5 0.1 constant_dynamic-slice_fusion.4
  230.6 2.2 gather_fusion
  232.8 1.4 fusion.52
  234.2 4.0 scatter_fusion
  238.2 3.1 fusion.22
  241.3 1.3 dynamic-slice.3
  243.3 0.9 scatter_custom_fusion.2
  244.2 76.1 %all-reduce = f32[2048]{0:T(1024)S(1)} all-reduce(f32[2048]{0:T(1024)S(1)} %bitcast.59), channel_id=2, replica_groups=mesh['row'=32,'col'=16] {'col'}, use_global_device_ids=true, to_apply=%region_2.3.clone | all-reduce | flops 2048 | bytes 16384
  320.4 0.1 fusion.35
  320.4 32.0 %reduce-scatter.3.cloned.1.call-done = bf16[128,256]{1,0:T(8,128)(2,1)} async-done(((bf16[2048,256]{1,0:T(8,128)(2,1)}), bf16[128,256]{1,0:T(8,128)(2,1)}) %reduce-scatter.3.cloned.1.call-update) | async-done | bytes 65552 | tf_op jit(solution)/shard_map/reduce_scatter | solution.py:93
  352.4 1.6 fusion.36
  354.1 0.7 multiply_convert_fusion.1
  354.8 69.4 %all-gather.5.cloned.1.call-done = bf16[2048,256]{1,0:T(8,128)(2,1)} async-done(((bf16[128,256]{1,0:T(8,128)(2,1)}), bf16[2048,256]{1,0:T(8,128)(2,1)}) %all-gather.5.cloned.1.call-update) | async-done | bytes 1048592 | tf_op jit(solution)/shard_map/all_gather | solution.py:101
  424.2 2.4 broadcast_in_dim.54
  426.7 13.4 %while.21 = (s32[]{:T(128)}, f32[32,128,256]{2,1,0:T(8,128)}, s32[]{:T(128)}, s32[88,2]{0,1:T(2,128)S(1)}, bf16[88,128,128]{1,2,0:T(8,128)(2,1)}, /*index=5*/s32...) while((s32[]{:T(128)}, f32[32,128,256]{2,1,0:T(8,128)}, ...), condition=%wide.region_12.13_spmd, body=%wide.region_10.12_spmd.sunk | while | flops 93177000 | bytes 8295165 | solution.py:35
  426.7 0.6 compare_convert_fusion.6
  427.3 0.1 constant_dynamic-slice_fusion.5
  427.4 0.6 gather_fusion.1
  428.0 1.4 fusion.56
  429.4 3.9 scatter_fusion.1
  433.3 0.6 compare_convert_fusion.6
  434.1 0.6 gather_fusion.1
  434.7 1.4 fusion.56
  436.1 4.0 scatter_fusion.1
  440.1 3.1 add_dynamic-update-slice_fusion
  443.2 3.7 convert_element_type.71
  447.0 147.7 %psum.15 = f32[256]{0:T(256)} all-reduce(f32[256]{0:T(256)S(1)} %get-tuple-element.134), channel_id=1, replica_groups=mesh['row'=32,'col'=16] {'row','col'}, use_global_device_ids=true, to_apply=%region_16.17 | all-reduce | flops 256 | bytes 2048 | tf_op jit(solution)/shard_map/psum | solution.py:127
  594.7 1.8 convolution_bitcast_fusion
  596.5 1.7 convolution_convert_fusion
  598.2 262.3 %all-reduce.4.cloned.1.call-done = f32[128,256]{0,1:T(8,128)} async-done(((f32[128,256]{0,1:T(8,128)}), f32[128,256]{0,1:T(8,128)}) %all-reduce.4.cloned.1.call-update) | async-done | bytes 131088 | tf_op jit(solution)/shard_map/psum | solution.py:127
  860.5 1.7 copy.16
  (39 shorter events, 0.5 us)
Async XLA Ops:
  7.2 147.7 %copy-start = (bf16[128,256]{1,0:T(8,128)(2,1)S(1)}, bf16[128,256]{1,0:T(8,128)(2,1)}, u32[]{:S(2)}) copy-start(bf16[128,256]{1,0:T(8,128)(2,1)} %param.12) | copy-start | bytes 196612
  7.2 212.9 %all-gather.3.cloned.1.call-start = ((), (), s32[]{:S(2)}) async-start(), calls=%async_computation.2 | async-start | bytes 2162688 | tf_op jit(solution)/shard_map/all_gather | solution.py:87
  12.0 209.6 %copy-start.2 = (bf16[1,88,128,128]{2,3,1,0:T(8,128)(2,1)}, bf16[1,88,128,128]{2,3,1,0:T(8,128)(2,1)S(1)}, u32[]{:S(2)}) copy-start(bf16[1,88,128,128]{2,3,1,0:T(8,128)(2,1)S(1)} %copy.14) | copy-start | bytes 8650756
  12.0 142.8 %copy-start.3 = (bf16[128,128]{1,0:T(8,128)(2,1)S(1)}, bf16[128,128]{1,0:T(8,128)(2,1)}, u32[]{:S(2)}) copy-start(bf16[128,128]{1,0:T(8,128)(2,1)} %param.11) | copy-start | bytes 98308
  12.0 209.6 %copy-start.4 = (s32[1,88,2]{1,2,0:T(2,128)S(1)}, s32[1,88,2]{1,2,0:T(2,128)}, u32[]{:S(2)}) copy-start(s32[1,88,2]{1,2,0:T(2,128)} %param.15) | copy-start | bytes 2116
  155.7 196.8 %reduce-scatter.3.cloned.1.call-start = ((), (), s32[]{:S(2)}) async-start(), calls=%async_computation.3 | async-start | bytes 1114112 | tf_op jit(solution)/shard_map/reduce_scatter | solution.py:93
  238.2 114.3 %copy-start.5 = (bf16[128,256]{1,0:T(8,128)(2,1)S(1)}, bf16[128,256]{1,0:T(8,128)(2,1)}, u32[]{:S(2)}) copy-start(bf16[128,256]{1,0:T(8,128)(2,1)} %param.17) | copy-start | bytes 196612
  238.2 114.3 %copy-start.6 = (f32[256]{0:T(256)S(1)}, f32[256]{0:T(256)}, u32[]{:S(2)}) copy-start(f32[256]{0:T(256)} %param.13) | copy-start | bytes 3076
  241.3 183.0 %all-gather.5.cloned.1.call-start = ((), (), s32[]{:S(2)}) async-start(), calls=%async_computation.4 | async-start | bytes 1114112 | tf_op jit(solution)/shard_map/all_gather | solution.py:101
  354.8 239.9 %reduce-scatter.5.cloned.1.call-start = ((), (), s32[]{:S(2)}) async-start(), calls=%async_computation.5 | async-start | bytes 2162688 | tf_op jit(solution)/shard_map/reduce_scatter | solution.py:114
  424.2 2.4 copy-start.1
  447.0 413.5 %all-reduce.4.cloned.1.call-start = ((), (), s32[]{:S(2)}) async-start(), calls=%async_computation.6 | async-start | bytes 262144 | tf_op jit(solution)/shard_map/psum | solution.py:127
Sparse Core Ops, SparseCore 0:
  155.8 64.2 all-gather.2
  241.4 110.9 reduce-scatter.2
  355.3 68.8 all-gather.4
  447.1 145.6 reduce-scatter.4
  598.9 261.5 all-reduce.3
where the time goes:
time: 870 us; the launch traced here: 869 us
  waiting for transfers between devices  428 us (49%)
  blocking collectives  363 us (42%)
  other arithmetic  34.3 us (4%)
  local copies, waits for them, and re-layouts  17.4 us (2%)
  between operations  15.9 us (2%)
  matrix products  9.82 us (1%)
    psum x1, waiting for transfers between devices, per_device(): lax.psum((weight_part, jnp.sum(grad_pre, axis=0)), ('row', 'col'))  262 us
    unnamed x2, blocking collectives  215 us
    psum x1, blocking collectives, per_device(): lax.psum((weight_part, jnp.sum(grad_pre, axis=0)), ('row', 'col'))  148 us
    all_gather x1, waiting for transfers between devices, per_device(): lax.all_gather((row_scale * grad_pre).astype(jnp.bfloat16), 'col', axis=0...  69.4 us
    all_gather x1, waiting for transfers between devices, per_device(): gathered = lax.all_gather(hidden, 'row', axis=0, tiled=True)  64.4 us
    reduce_scatter x1, waiting for transfers between devices, per_device(): lax.psum_scatter((running + jnp.where(diagonal, own_rows, 0.0)).astype(jn...  32 us
  transfers between devices with their start and end apart: 5, of which 4 were waited for; matrix products, arithmetic and copies ran while one was open for 0% of the time, Pallas kernels for 0%

commit v1 on v0

v1 whole, which is shorter than its diff:
```python
import jax
import jax.numpy as jnp
from jax import lax
from jax.experimental import pallas as pl
from jax.experimental.pallas import tpu as pltpu
from jax.sharding import PartitionSpec as P


BLK = 128
GROUP = 4
F32 = jnp.float32
BF16 = jnp.bfloat16
VMEM = pl.BlockSpec(memory_space=pltpu.VMEM)
SMEM = pl.BlockSpec(memory_space=pltpu.SMEM)
NT = (((1,), (1,)), ((), ()))
TN = (((0,), (0,)), ((), ()))


def call(kernel, name, operands, specs, outs, scratch=(), flops=0, limit=32):
    single = not isinstance(outs, (list, tuple))
    moved = sum(x.size * x.dtype.itemsize for x in operands)
    moved += sum(
        o.dtype.itemsize * _size(o.shape) for o in ([outs] if single else outs)
    )
    return pl.pallas_call(
        kernel,
        out_shape=outs,
        in_specs=specs,
        out_specs=VMEM if single else [VMEM] * len(outs),
        scratch_shapes=list(scratch),
        compiler_params=pltpu.CompilerParams(vmem_limit_bytes=limit << 20),
        cost_estimate=pl.CostEstimate(flops=flops, bytes_accessed=moved, transcendentals=0),
        name=name,
    )(*operands)


def _size(shape):
    total = 1
    for n in shape:
        total *= n
    return total


def struct(shape, dtype):
    return jax.ShapeDtypeStruct(shape, dtype)


def split(value):
    high = value.astype(BF16).astype(F32)
    return high, value - high


def slot_of(q, parity, half):
    return ((q & 1) ^ parity) * half + (q >> 1)


def eye(n):
    return lax.broadcasted_iota(jnp.int32, (n, n), 0) == lax.broadcasted_iota(jnp.int32, (n, n), 1)


def count_kernel(info, coords, tiles, own, other, rows, col_acc, row_acc):
    half = own.shape[0]
    col_acc[...] = jnp.zeros_like(col_acc)
    row_acc[...] = jnp.zeros_like(row_acc)
    count, parity = info[0], info[1]
    ones = jnp.ones((8, BLK), BF16)

    def group(g, carry):
        for u in range(GROUP):
            s = g * GROUP + u
            live = jnp.where(s < count, 1.0, 0.0).astype(F32)
            tile = tiles[s]
            column = jnp.sum(tile.reshape(BLK // 16, 16, BLK), axis=0)
            line = lax.dot_general(ones, tile, NT, preferred_element_type=F32)
            at = slot_of(coords[s, 1], parity, half)
            col_acc[at] += column.astype(F32) * live
            row_acc[coords[s, 0]] += line * live
        return carry

    lax.fori_loop(0, (count + GROUP - 1) // GROUP, group, 0)
    total = jnp.sum(col_acc[...], axis=1)
    own[...] = total[:half]
    other[...] = total[half:]
    rows[...] = jnp.max(row_acc[...], axis=1)


def whole_parts(total):
    high = jnp.floor(total * (1.0 / 256.0)) * 256.0
    return high, total - high


def piece_kernel(x, own, arrived, message):
    half = own.shape[0]
    high, low = whole_parts(own[...] + arrived[...])
    counts = jnp.concatenate([high, low], axis=0).astype(BF16)
    for k in range(half):
        message[k, :BLK] = x[...]
        message[k, BLK:] = counts


def scale_kernel(message, scaled, scale):
    half = scaled.shape[0]
    degree = 1.0 + jnp.sum(
        message[:, BLK : BLK + half].astype(F32) + message[:, BLK + half :].astype(F32), axis=0
    )
    factor = lax.rsqrt(degree)
    scale[...] = factor
    turned = lax.dot_general(
        eye(BLK).astype(F32), factor, NT, precision=lax.Precision.HIGHEST, preferred_element_type=F32
    )
    for k in range(half):
        scaled[k] = (message[k, :BLK].astype(F32) * turned[:, k : k + 1]).astype(BF16)


def forward_kernel(info, coords, tiles, own, other, rows, message, features, acc):
    half, row_blocks = own.shape[0], message.shape[0]
    count, parity, diagonal = info[0], info[1], info[2]
    features[:half] = own[...]
    features[half:] = other[...]

    @pl.when(diagonal == 1)
    def _():
        for p in range(row_blocks):
            acc[p] = features[slot_of(parity * row_blocks + p, parity, half)].astype(F32)

    @pl.when(diagonal == 0)
    def _():
        acc[...] = jnp.zeros_like(acc)

    def group(g, carry):
        for u in range(GROUP):
            s = g * GROUP + u
            live = jnp.where(s < count, 1.0, 0.0).astype(F32)
            source = features[slot_of(coords[s, 1], parity, half)]
            product = jnp.dot(tiles[s], source, preferred_element_type=F32)
            acc[coords[s, 0]] += product * live
        return carry

    lax.fori_loop(0, (count + GROUP - 1) // GROUP, group, 0)
    line = lax.broadcasted_iota(jnp.int32, (16, BLK), 0)
    for p in range(row_blocks):
        message[p, :BLK] = acc[p].astype(BF16)
        high, low = whole_parts(rows[p : p + 1])
        extra = jnp.where(line == 0, high, jnp.where(line == 1, low, 0.0))
        message[p, BLK:] = extra.astype(BF16)


def node_kernel(partials, weight, bias, cotangent, activations, sent, grads):
    parts = grads.shape[0]
    chunk = BLK // parts
    total = jnp.sum(partials[...].astype(F32), axis=0)
    summed = total[:BLK]
    degree = 1.0 + total[BLK : BLK + 1] + total[BLK + 1 : BLK + 2]
    scale = jnp.sum(jnp.where(eye(BLK), lax.rsqrt(degree), 0.0), axis=1, keepdims=True)
    high, low = split(summed)
    high, low = high.astype(BF16), low.astype(BF16)
    product = jnp.dot(high, weight[...], preferred_element_type=F32)
    product += jnp.dot(low, weight[...], preferred_element_type=F32)
    pre = scale * product + bias[...]
    sigmoid = jax.nn.sigmoid(pre)
    activations[...] = (pre * sigmoid).astype(BF16)
    grad_pre = cotangent[...].astype(F32) * sigmoid * (1.0 + pre * (1.0 - sigmoid))
    back = (scale * grad_pre).astype(BF16)
    sent[...] = lax.dot_general(weight[...], back, NT, preferred_element_type=F32).astype(BF16)
    grad = lax.dot_general(high, back, TN, preferred_element_type=F32)
    grad += lax.dot_general(low, back, TN, preferred_element_type=F32)
    grad_bias = jnp.sum(grad_pre, axis=0, keepdims=True)
    line = lax.broadcasted_iota(jnp.int32, (8, BLK), 0)
    extra = jnp.where(
        line == 0, grad_bias[:, :BLK], jnp.where(line == 1, grad_bias[:, BLK:], 0.0)
    )
    for k in range(parts):
        grads[k, :chunk] = grad[k * chunk : (k + 1) * chunk, :BLK]
        grads[k, chunk : 2 * chunk] = grad[k * chunk : (k + 1) * chunk, BLK:]
        grads[k, 2 * chunk :] = extra


def mix_kernel(grads, sent, message):
    high, low = split(jnp.sum(grads[...], axis=0))
    tail = jnp.concatenate([high, low], axis=0).astype(BF16)
    for c in range(message.shape[0]):
        message[c, :BLK] = sent[...]
        message[c, BLK:] = tail


def backward_kernel(info, coords, tiles, message, own, other, acc):
    half, row_blocks = own.shape[0], message.shape[0]
    count, parity, diagonal = info[0], info[1], info[2]
    acc[...] = jnp.zeros_like(acc)

    @pl.when(diagonal == 1)
    def _():
        for p in range(row_blocks):
            acc[slot_of(parity * row_blocks + p, parity, half)] = message[p, :BLK].astype(F32)

    def group(g, carry):
        for u in range(GROUP):
            s = g * GROUP + u
            live = jnp.where(s < count, 1.0, 0.0).astype(F32)
            product = jnp.dot(message[coords[s, 0], :BLK], tiles[s], preferred_element_type=F32)
            acc[slot_of(coords[s, 1], parity, half)] += product * live
        return carry

    lax.fori_loop(0, (count + GROUP - 1) // GROUP, group, 0)
    own[...] = acc[:half].astype(BF16)
    for k in range(half):
        other[k * BLK : (k + 1) * BLK] = acc[half + k].astype(BF16)
    tail = jnp.sum(message[:, BLK:].astype(F32), axis=0)
    size = tail.shape[0] // 2
    high, low = split(tail[:size] + tail[size:])
    other[half * BLK :] = jnp.concatenate([high, low], axis=0).astype(BF16)


def pair_kernel(partials, own, arrived, message, grad_bias):
    half = own.shape[0]
    tail = jnp.sum(partials[:, BLK:].astype(F32), axis=0)
    size = tail.shape[0] // 2
    high, low = split(tail[:size] + tail[size:])
    mine = high + low.astype(BF16).astype(F32)
    theirs = arrived[half * BLK :].astype(F32)
    total = mine + theirs[:size] + theirs[size:]
    grad_bias[...] = total[size - 8 :]
    high, low = split(total[: size - 8])
    extra = jnp.concatenate([high, low], axis=0).astype(BF16)
    for k in range(half):
        message[k, :BLK] = (
            own[k].astype(F32) + arrived[k * BLK : (k + 1) * BLK].astype(F32)
        ).astype(BF16)
        message[k, BLK:] = extra


def last_kernel(info, message, scale, grad_inputs, grad_weight):
    half = message.shape[0]
    chunk = BLK // half
    total = jnp.sum(message[:, :BLK].astype(F32), axis=0)
    total = total * scale[pl.ds(info[3], 1), :]
    grad_inputs[...] = total.T.astype(BF16)
    for k in range(half):
        tail = message[k, BLK:].astype(F32)
        tail = tail[: 2 * chunk] + tail[2 * chunk :]
        grad_weight[k * chunk : (k + 1) * chunk, :BLK] = tail[:chunk]
        grad_weight[k * chunk : (k + 1) * chunk, BLK:] = tail[chunk:]


def per_device(node_inputs, weight, bias, edge_tiles, block_coords, block_counts, out_cotangent):
    row_devices = lax.axis_size("row")
    row_blocks = lax.axis_size("col")
    half = row_devices // 2
    slots = edge_tiles.shape[1]
    tiles = edge_tiles[0]
    coords = block_coords[0]
    row_index = lax.axis_index("row")
    col_index = lax.axis_index("col")
    diagonal = (col_index == row_index // (row_devices // row_blocks)).astype(jnp.int32)
    info = jnp.stack([block_counts[0, 0], row_index % 2, diagonal, row_index // 2])
    parities = [[2 * k + h for k in range(half)] for h in range(2)]
    partner = [(i, i ^ 1) for i in range(row_devices)]
    work = 2 * slots * BLK**3

    own_count, other_count, row_count = call(
        count_kernel,
        "count",
        (info, coords, tiles),
        [SMEM, SMEM, VMEM],
        [struct((half, BLK), F32), struct((half, BLK), F32), struct((row_blocks, BLK), F32)],
        [pltpu.VMEM((row_devices, 16, BLK), F32), pltpu.VMEM((row_blocks, 8, BLK), F32)],
        work // 16,
    )
    arrived = lax.ppermute(other_count, "row", partner)
    message = call(
        piece_kernel,
        "piece",
        (node_inputs, own_count, arrived),
        [VMEM] * 3,
        struct((half, BLK + 2 * half, BLK), BF16),
    )
    message = lax.all_to_all(message, "row", 0, 0, tiled=True, axis_index_groups=parities)
    scaled, scale = call(
        scale_kernel,
        "scale",
        (message,),
        [VMEM],
        [struct((half, BLK, BLK), BF16), struct((half, BLK), F32)],
    )
    scaled_other = lax.ppermute(scaled, "row", partner)
    message = call(
        forward_kernel,
        "forward",
        (info, coords, tiles, scaled, scaled_other, row_count),
        [SMEM, SMEM] + [VMEM] * 4,
        struct((row_blocks, BLK + 16, BLK), BF16),
        [pltpu.VMEM((row_devices, BLK, BLK), BF16), pltpu.VMEM((row_blocks, BLK, BLK), F32)],
        work,
    )
    message = lax.all_to_all(message, "col", 0, 0, tiled=True)
    width = weight.shape[1]
    chunk_rows = 2 * (BLK // half) + 8
    activations, sent, grads = call(
        node_kernel,
        "node",
        (message, weight, bias.reshape(1, width), out_cotangent),
        [VMEM] * 4,
        [
            struct((BLK, width), BF16),
            struct((BLK, BLK), BF16),
            struct((half, chunk_rows, BLK), F32),
        ],
        (),
        8 * BLK * BLK * width,
    )
    grads = lax.all_to_all(grads, "row", 0, 0, tiled=True, axis_index_groups=parities)
    message = call(
        mix_kernel,
        "mix",
        (grads, sent),
        [VMEM] * 2,
        struct((row_blocks, BLK + 2 * chunk_rows, BLK), BF16),
    )
    message = lax.all_to_all(message, "col", 0, 0, tiled=True)
    own, other = call(
        backward_kernel,
        "backward",
        (info, coords, tiles, message),
        [SMEM, SMEM, VMEM, VMEM],
        [struct((half, BLK, BLK), BF16), struct((half * BLK + 2 * chunk_rows, BLK), BF16)],
        [pltpu.VMEM((row_devices, BLK, BLK), F32)],
        work,
    )
    arrived = lax.ppermute(other, "row", partner)
    message, grad_bias = call(
        pair_kernel,
        "pair",
        (message, own, arrived),
        [VMEM] * 3,
        [struct((half, BLK + 4 * (BLK // half), BLK), BF16), struct((8, BLK), F32)],
    )
    message = lax.all_to_all(message, "row", 0, 0, tiled=True, axis_index_groups=parities)
    grad_inputs, grad_weight = call(
        last_kernel,
        "last",
        (info, message, scale),
        [SMEM, VMEM, VMEM],
        [struct((BLK, BLK), BF16), struct((BLK, width), F32)],
    )
    return activations, grad_inputs, grad_weight, grad_bias[:2].reshape(width)


def solution(mesh):
    in_specs = (
        P(("col", "row"), None),
        P(),
        P(),
        P("row", "col", None, None),
        P("row", "col", None),
        P("row", "col"),
        P(("row", "col"), None),
    )
    out_specs = (P(("row", "col"), None), P(("col", "row"), None), P(), P())
    return jax.shard_map(
        per_device, mesh=mesh, in_specs=in_specs, out_specs=out_specs, check_vma=False
    )
```

time: 870 us -> 160 us (0.18)
  the two profiles are of different devices: /device:TPU:1 before, /device:TPU:8 now
where the time goes in v1:
time: 160 us
  blocking collectives  102 us (64%)
  waiting for transfers between devices  25 us (16%)
  starting transfers between devices  17.7 us (11%)
  Pallas kernels  10 us (6%)
  local copies, waits for them, and re-layouts  3.18 us (2%)
    all_to_all x2, blocking collectives, per_device(): message = lax.all_to_all(message, 'col', 0, 0, tiled=True)  58.3 us
    all_to_all x1, blocking collectives, per_device(): lax.all_to_all(message, 'row', 0, 0, tiled=True, axis_index_groups=parities)  28.6 us
    all_to_all x1, waiting for transfers between devices, per_device(): lax.all_to_all(message, 'row', 0, 0, tiled=True, axis_index_groups=parities)  20.8 us
    all_to_all x1, blocking collectives, per_device(): lax.all_to_all(grads, 'row', 0, 0, tiled=True, axis_index_groups=parities)  15.3 us
    pallas_call x9, Pallas kernels, call(): pl.pallas_call(kernel, out_shape=outs, in_specs=specs, out_specs=VMEM if...  10 us
    all_to_all x1, starting transfers between devices, per_device(): lax.all_to_all(message, 'row', 0, 0, tiled=True, axis_index_groups=parities)  6.91 us
    ppermute x1, starting transfers between devices, per_device(): arrived = lax.ppermute(other_count, 'row', partner)  5.3 us
    ppermute x1, starting transfers between devices, per_device(): arrived = lax.ppermute(other, 'row', partner)  3.44 us
  transfers between devices with their start and end apart: 4, of which 4 were waited for; matrix products, arithmetic and copies ran while one was open for 0% of the time, Pallas kernels for 0%

profile of v1, /device:TPU:8, one launch (start us, length us, event | category | flops | bytes accessed | tf_op | source)
XLA Modules:
  0.0 159.6 jit_solution(15784425673638505065)
XLA Ops:
  0.6 0.0 copy-start.4
  1.3 0.8 copy.11
  2.1 0.1 pad_add_fusion.info
  2.2 0.0 copy-start
  2.2 1.8 %copy-done = bf16[1,88,128,128]{3,2,1,0:T(8,128)(2,1)S(1)} copy-done((bf16[1,88,128,128]{3,2,1,0:T(8,128)(2,1)S(1)}, bf16[1,88,128,128]{3,2,1,0:T(8,128)(2,1)}, u32[]{:S(2)}) %copy-start) | copy-done | bytes 2883608
  4.0 0.0 copy-start.1
  4.0 1.9 %count.1 = (f32[16,128]{1,0:T(8,128)S(1)}, f32[16,128]{1,0:T(8,128)S(1)}, f32[16,128]{1,0:T(8,128)S(1)}) custom-call(s32[4]{0:T(128)S(1)} %pad_add_fusion.info, s32[88,2]{1,0:T(8,128)S(1)} %bitcast.13, bf16[88,128,128]{2,1,0:T(8,128)(2,1)S(1)} %bitcast.10), custom_call_target="tpu_custom_call" | custom-call | flops 23068672 | bytes 2908880 | tf_op jit(solution)/shard_map/count/pallas_call | solution.py:25
  5.9 5.3 %collective-permute-start = (f32[16,128]{1,0:T(8,128)S(1)}, f32[16,128]{1,0:T(8,128)S(1)}, u32[]{:S(2)}, u32[]{:S(2)}) collective-permute-start(f32[16,128]{1,0:T(8,128)S(1)} %get-tuple-element.19), channel_id=1, source_target_pairs={{0,16},{16,0},{32,48},{48,32},{64,80},{80,64},{96,112},{112,96},{1... | collective-permute-start | bytes 24584 | tf_op jit(solution)/shard_map/ppermute | solution.py:269
  11.2 0.8 collective-permute-done.arrived
  12.0 0.0 copy-done.4
  12.0 0.1 piece.1
  12.1 28.6 %all_to_all.25.message = bf16[16,160,128]{2,1,0:T(8,128)(2,1)S(1)} all-to-all(bf16[16,160,128]{2,1,0:T(8,128)(2,1)S(1)} %piece.1), channel_id=1, replica_groups={{0,32,64,96,128,160,192,224,256,288,320,352,384,416,448,480},{16,48,80,..., dimensions={0} | all-to-all | bytes 1310720 | tf_op jit(solution)/shard_map/all_to_all | solution.py:277
  40.7 0.6 scale.1
  41.3 0.0 copy-start.2
  41.3 0.0 copy-start.3
  41.3 0.0 copy-start.5
  41.3 2.1 %collective-permute-start.1 = (bf16[16,128,128]{2,1,0:T(8,128)(2,1)S(1)}, bf16[16,128,128]{2,1,0:T(8,128)(2,1)S(1)}, u32[]{:S(2)}, u32[]{:S(2)}) collective-permute-start(bf16[16,128,128]{2,1,0:T(8,128)(2,1)S(1)} %get-tuple-element.20.own), channel_id=1, source_target_pairs={{0,16},{16,0},{32,48},{48,32},{64,80},{80,64},{96,112},{112,96},{1... | collective-permute-start | bytes 1572872 | tf_op jit(solution)/shard_map/ppermute | solution.py:285
  43.4 1.9 %collective-permute-done.1.other = bf16[16,128,128]{2,1,0:T(8,128)(2,1)S(1)} collective-permute-done((bf16[16,128,128]{2,1,0:T(8,128)(2,1)S(1)}, bf16[16,128,128]{2,1,0:T(8,128)(2,1)S(1)}, u32[]{:S(2)}, u32[]{:S(2)}) %collective-permute-start.1) | collective-permute-done | bytes 524320 | tf_op jit(solution)/shard_map/ppermute | solution.py:285
  45.2 0.0 copy-done.1
  45.3 2.1 %forward.1 = bf16[16,144,128]{2,1,0:T(8,128)(2,1)S(1)} custom-call(s32[4]{0:T(128)S(1)} %pad_add_fusion.info, s32[88,2]{1,0:T(8,128)S(1)} %bitcast.14, bf16[88,128,128]{2,1,0:T(8,128)(2,1)S(1)} %bitcast.11, bf16[16,128,128]{2,1,0:T(8,128)(2,1)S(1)} %get-tuple-element.20.own, bf16[16,128,128]{2,1,0:T(8,128)(2,1)S(1)} %collective-permute-done.1.other, ...), custom_call_target="tpu_custom_call" | custom-call | flops 369098752 | bytes 4530896 | tf_op jit(solution)/shard_map/forward/pallas_call | solution.py:25
  47.3 35.4 %all_to_all.26.partials = bf16[16,144,128]{2,1,0:T(8,128)(2,1)S(1)} all-to-all(bf16[16,144,128]{2,1,0:T(8,128)(2,1)S(1)} %forward.1), channel_id=1, replica_groups=mesh['row'=32,'col'=16] {'col'}, dimensions={0} | all-to-all | bytes 1179648 | tf_op jit(solution)/shard_map/all_to_all | solution.py:295
  82.7 0.0 copy-done.2
  82.7 0.0 copy-done.3
  82.7 0.0 copy-done.5
  82.7 0.9 node.1
  83.6 15.3 %all_to_all.27.grads = f32[16,24,128]{2,1,0:T(8,128)S(1)} all-to-all(f32[16,24,128]{2,1,0:T(8,128)S(1)} %get-tuple-element.23), channel_id=1, replica_groups={{0,32,64,96,128,160,192,224,256,288,320,352,384,416,448,480},{16,48,80,..., dimensions={0} | all-to-all | bytes 393216 | tf_op jit(solution)/shard_map/all_to_all | solution.py:311
  98.9 0.1 mix.1
  99.0 22.9 %all_to_all.28.message.partials = bf16[16,176,128]{2,1,0:T(8,128)(2,1)S(1)} all-to-all(bf16[16,176,128]{2,1,0:T(8,128)(2,1)S(1)} %mix.1), channel_id=1, replica_groups=mesh['row'=32,'col'=16] {'col'}, dimensions={0} | all-to-all | bytes 1441792 | tf_op jit(solution)/shard_map/all_to_all | solution.py:319
  121.9 2.1 %backward.1 = (bf16[16,128,128]{2,1,0:T(8,128)(2,1)S(1)}, bf16[2096,128]{1,0:T(8,128)(2,1)S(1)}) custom-call(s32[4]{0:T(128)S(1)} %pad_add_fusion.info, s32[88,2]{1,0:T(8,128)S(1)} %bitcast.15, bf16[88,128,128]{2,1,0:T(8,128)(2,1)S(1)} %bitcast.12, bf16[16,176,128]{2,1,0:T(8,128)(2,1)S(1)} %all_to_all.28.message.partials), custom_call_target="tpu_custom_call" | custom-call | flops 369098752 | bytes 4666064 | tf_op jit(solution)/shard_map/backward/pallas_call | solution.py:25
  124.0 3.4 %collective-permute-start.2 = (bf16[2096,128]{1,0:T(8,128)(2,1)S(1)}, bf16[2096,128]{1,0:T(8,128)(2,1)S(1)}, u32[]{:S(2)}, u32[]{:S(2)}) collective-permute-start(bf16[2096,128]{1,0:T(8,128)(2,1)S(1)} %get-tuple-element.26), channel_id=1, source_target_pairs={{0,16},{16,0},{32,48},{48,32},{64,80},{80,64},{96,112},{112,96},{1... | collective-permute-start | bytes 1609736 | tf_op jit(solution)/shard_map/ppermute | solution.py:329
  127.5 1.5 collective-permute-done.2.arrived
  129.0 1.0 pair.1
  130.0 6.9 %all-to-all-start.4 = ((bf16[16,160,128]{2,1,0:T(8,128)(2,1)}), bf16[16,160,128]{2,1,0:T(8,128)(2,1)S(1)}, u32[]{:S(2)}, u32[]{:S(2)}) async-start(bf16[16,160,128]{2,1,0:T(8,128)(2,1)} %get-tuple-element.27), calls=%async_computation.4 | async-start | bytes 1310720 | tf_op jit(solution)/shard_map/all_to_all | solution.py:337
  136.9 0.6 slice_bitcast_fusion
  137.5 20.8 %all-to-all-done.4.message = bf16[16,160,128]{2,1,0:T(8,128)(2,1)S(1)} async-done(((bf16[16,160,128]{2,1,0:T(8,128)(2,1)}), bf16[16,160,128]{2,1,0:T(8,128)(2,1)S(1)}, u32[]{:S(2)}, u32[]{:S(2)}) %all-to-all-start.4) | async-done | bytes 655392 | tf_op jit(solution)/shard_map/all_to_all | solution.py:337
  158.3 1.3 last.1
Async XLA Ops:
  0.6 11.4 %copy-start.4 = (bf16[128,128]{1,0:T(8,128)(2,1)S(1)}, bf16[128,128]{1,0:T(8,128)(2,1)}, u32[]{:S(2)}) copy-start(bf16[128,128]{1,0:T(8,128)(2,1)} %x.1) | copy-start | bytes 98308
  2.2 1.8 %copy-start = (bf16[1,88,128,128]{3,2,1,0:T(8,128)(2,1)S(1)}, bf16[1,88,128,128]{3,2,1,0:T(8,128)(2,1)}, u32[]{:S(2)}) copy-start(bf16[1,88,128,128]{3,2,1,0:T(8,128)(2,1)} %param.10) | copy-start | bytes 8650756
  4.0 41.3 %copy-start.1 = (bf16[1,88,128,128]{3,2,1,0:T(8,128)(2,1)S(1)}, bf16[1,88,128,128]{3,2,1,0:T(8,128)(2,1)}, u32[]{:S(2)}) copy-start(bf16[1,88,128,128]{3,2,1,0:T(8,128)(2,1)} %param.10) | copy-start | bytes 8650756
  5.9 6.1 %collective-permute-start = (f32[16,128]{1,0:T(8,128)S(1)}, f32[16,128]{1,0:T(8,128)S(1)}, u32[]{:S(2)}, u32[]{:S(2)}) collective-permute-start(f32[16,128]{1,0:T(8,128)S(1)} %get-tuple-element.19), channel_id=1, source_target_pairs={{0,16},{16,0},{32,48},{48,32},{64,80},{80,64},{96,112},{112,96},{1... | collective-permute-start | bytes 24584 | tf_op jit(solution)/shard_map/ppermute | solution.py:269
  41.3 41.4 %copy-start.2 = (bf16[128,256]{1,0:T(8,128)(2,1)S(1)}, bf16[128,256]{1,0:T(8,128)(2,1)}, u32[]{:S(2)}) copy-start(bf16[128,256]{1,0:T(8,128)(2,1)} %weight.1) | copy-start | bytes 196612
  41.3 41.4 %copy-start.3 = (bf16[128,256]{1,0:T(8,128)(2,1)S(1)}, bf16[128,256]{1,0:T(8,128)(2,1)}, u32[]{:S(2)}) copy-start(bf16[128,256]{1,0:T(8,128)(2,1)} %cotangent.1) | copy-start | bytes 196612
  41.3 41.4 %copy-start.5 = (f32[256]{0:T(256)S(1)}, f32[256]{0:T(256)}, u32[]{:S(2)}) copy-start(f32[256]{0:T(256)} %param.9) | copy-start | bytes 3076
  41.3 3.9 %collective-permute-start.1 = (bf16[16,128,128]{2,1,0:T(8,128)(2,1)S(1)}, bf16[16,128,128]{2,1,0:T(8,128)(2,1)S(1)}, u32[]{:S(2)}, u32[]{:S(2)}) collective-permute-start(bf16[16,128,128]{2,1,0:T(8,128)(2,1)S(1)} %get-tuple-element.20.own), channel_id=1, source_target_pairs={{0,16},{16,0},{32,48},{48,32},{64,80},{80,64},{96,112},{112,96},{1... | collective-permute-start | bytes 1572872 | tf_op jit(solution)/shard_map/ppermute | solution.py:285
  124.0 5.0 %collective-permute-start.2 = (bf16[2096,128]{1,0:T(8,128)(2,1)S(1)}, bf16[2096,128]{1,0:T(8,128)(2,1)S(1)}, u32[]{:S(2)}, u32[]{:S(2)}) collective-permute-start(bf16[2096,128]{1,0:T(8,128)(2,1)S(1)} %get-tuple-element.26), channel_id=1, source_target_pairs={{0,16},{16,0},{32,48},{48,32},{64,80},{80,64},{96,112},{112,96},{1... | collective-permute-start | bytes 1609736 | tf_op jit(solution)/shard_map/ppermute | solution.py:329
  130.0 28.3 %all-to-all-start.4 = ((bf16[16,160,128]{2,1,0:T(8,128)(2,1)}), bf16[16,160,128]{2,1,0:T(8,128)(2,1)S(1)}, u32[]{:S(2)}, u32[]{:S(2)}) async-start(bf16[16,160,128]{2,1,0:T(8,128)(2,1)} %get-tuple-element.27), calls=%async_computation.4 | async-start | bytes 1310720 | tf_op jit(solution)/shard_map/all_to_all | solution.py:337

commit v2 on v1

v2 whole, which is shorter than its diff:
```python
import jax
import jax.numpy as jnp
from jax import lax
from jax.experimental import pallas as pl
from jax.experimental.pallas import tpu as pltpu
from jax.sharding import PartitionSpec as P


BLK = 128
GROUP = 4
UNROLL = 2
PARTS = 4
CODE = 6
MASK = (1 << CODE) - 1
ROW_PAIRS = 4
COL_PAIRS = 3
F32 = jnp.float32
BF16 = jnp.bfloat16
VMEM = pl.BlockSpec(memory_space=pltpu.VMEM)
SMEM = pl.BlockSpec(memory_space=pltpu.SMEM)
NT = (((1,), (1,)), ((), ()))
TN = (((0,), (0,)), ((), ()))


def call(kernel, name, operands, specs, outs, scratch=(), flops=0, limit=32, out_specs=None):
    single = not isinstance(outs, (list, tuple))
    moved = sum(x.size * x.dtype.itemsize for x in operands)
    moved += sum(
        o.dtype.itemsize * _size(o.shape) for o in ([outs] if single else outs)
    )
    return pl.pallas_call(
        kernel,
        out_shape=outs,
        in_specs=specs,
        out_specs=out_specs or (VMEM if single else [VMEM] * len(outs)),
        scratch_shapes=list(scratch),
        compiler_params=pltpu.CompilerParams(vmem_limit_bytes=limit << 20),
        cost_estimate=pl.CostEstimate(flops=flops, bytes_accessed=moved, transcendentals=0),
        name=name,
    )(*operands)


def _size(shape):
    total = 1
    for n in shape:
        total *= n
    return total


def struct(shape, dtype):
    return jax.ShapeDtypeStruct(shape, dtype)


def split(value):
    high = value.astype(BF16).astype(F32)
    return high, value - high


def slot_of(q, parity, half):
    return ((q & 1) ^ parity) * half + (q >> 1)


def eye(n):
    return lax.broadcasted_iota(jnp.int32, (n, n), 0) == lax.broadcasted_iota(jnp.int32, (n, n), 1)


def count_kernel(info, coords, tiles, x, message, held, col_acc, arrivals):
    col_acc[...] = jnp.zeros_like(col_acc)
    count, parity = info[0], info[1]
    half = col_acc.shape[0] // 2
    part = held.shape[0] // PARTS
    copies = [
        pltpu.make_async_copy(
            tiles.at[pl.ds(i * part, part)], held.at[pl.ds(i * part, part)], arrivals.at[i]
        )
        for i in range(PARTS)
    ]
    for copy in copies:
        copy.start()

    def group(g, carry):
        for u in range(UNROLL):
            s = g * UNROLL + u
            live = jnp.where(s < count, 1.0, 0.0).astype(F32)
            column = jnp.sum(held[s].reshape(BLK // 16, 16, BLK), axis=0)
            col_acc[slot_of(coords[s, 1], parity, half)] += column.astype(F32) * live
        return carry

    for i, copy in enumerate(copies):
        copy.wait()
        first = i * part // UNROLL
        last = jnp.minimum((count + UNROLL - 1) // UNROLL, (i + 1) * part // UNROLL)
        lax.fori_loop(first, last, group, 0)
    total = jnp.sum(col_acc[...], axis=1)
    even = jnp.where(parity == 0, total[:half], total[half:])
    odd = jnp.where(parity == 0, total[half:], total[:half])
    total = jnp.concatenate([even, odd], axis=0).astype(BF16)
    for k in range(half):
        message[k, :BLK] = x[...]
        message[k, BLK:] = total


def plan_kernel(info, coords, tiles, rows, plan, row_acc):
    row_blocks = rows.shape[0]
    row_devices = (plan.shape[0] - 2 - row_blocks) // (2 * row_blocks + 1)
    half = row_devices // 2
    second = row_blocks * row_devices
    lengths = 2 * second
    longest = lengths + row_blocks + row_devices
    count, parity = info[0], info[1]

    def blank(i, carry):
        plan[i] = row_devices
        plan[second + i] = row_blocks
        return carry

    lax.fori_loop(0, second, blank, 0, unroll=8)
    for i in range(row_blocks + row_devices + 2):
        plan[lengths + i] = 0

    def enter(s, carry):
        p = coords[s, 0]
        slot = slot_of(coords[s, 1], parity, half)
        at_row, at_col = lengths + p, lengths + row_blocks + slot
        n_row, n_col = plan[at_row], plan[at_col]
        plan[p * row_devices + n_row] = (s << CODE) + slot
        plan[second + slot * row_blocks + n_col] = (s << CODE) + p
        plan[at_row] = n_row + 1
        plan[at_col] = n_col + 1
        return jnp.maximum(carry[0], n_row + 1), jnp.maximum(carry[1], n_col + 1)

    top_row, top_col = lax.fori_loop(0, count, enter, (jnp.int32(0), jnp.int32(0)))
    plan[longest] = top_row
    plan[longest + 1] = top_col

    row_acc[...] = jnp.zeros_like(row_acc)
    ones = jnp.ones((8, BLK), BF16)

    def group(g, carry):
        for u in range(GROUP):
            s = g * GROUP + u
            live = jnp.where(s < count, 1.0, 0.0).astype(F32)
            line = lax.dot_general(ones, tiles[s], NT, preferred_element_type=F32)
            row_acc[coords[s, 0]] += line * live
        return carry

    lax.fori_loop(0, (count + GROUP - 1) // GROUP, group, 0)
    rows[...] = jnp.max(row_acc[...], axis=1)


def whole_parts(total):
    high = jnp.floor(total * (1.0 / 256.0)) * 256.0
    return high, total - high


def forward_kernel(info, plan, tiles, own, other, rows, message, scale, features, acc):
    half, row_blocks = own.shape[0], message.shape[0]
    parity, diagonal = info[1], info[2]
    degree = 1.0 + jnp.sum(own[:, BLK:].astype(F32) + other[:, BLK:].astype(F32), axis=0)
    factor = lax.rsqrt(degree)
    scale[...] = factor
    turned = lax.dot_general(
        eye(BLK).astype(F32), factor, NT, precision=lax.Precision.HIGHEST, preferred_element_type=F32
    )
    even, odd = turned[:, :half], turned[:, half:]
    mine = jnp.where(parity == 0, even, odd)
    theirs = jnp.where(parity == 0, odd, even)
    for k in range(half):
        features[k] = (own[k, :BLK].astype(F32) * mine[:, k : k + 1]).astype(BF16)
        features[half + k] = (other[k, :BLK].astype(F32) * theirs[:, k : k + 1]).astype(BF16)

    row_devices = 2 * half
    features[row_devices] = jnp.zeros((BLK, BLK), BF16)
    lengths = 2 * row_blocks * row_devices

    def pair(p, j):
        first, second = plan[p * row_devices + 2 * j], plan[p * row_devices + 2 * j + 1]
        left = jnp.concatenate([tiles[first >> CODE], tiles[second >> CODE]], axis=1)
        right = jnp.concatenate([features[first & MASK], features[second & MASK]], axis=0)
        return jnp.dot(left, right, preferred_element_type=F32)

    fixed = min(ROW_PAIRS, half)
    for p in range(row_blocks):
        same = features[slot_of(parity * row_blocks + p, parity, half)].astype(F32)
        total = jnp.where(diagonal == 1, same, 0.0)
        for j in range(fixed):
            total += pair(p, j)
        acc[p] = total

    @pl.when(plan[lengths + row_blocks + row_devices] > 2 * fixed)
    def _():
        for p in range(row_blocks):

            def more(j, carry):
                acc[p] += pair(p, j)
                return carry

            lax.fori_loop(fixed, (plan[lengths + p] + 1) // 2, more, 0)

    line = lax.broadcasted_iota(jnp.int32, (16, BLK), 0)
    for p in range(row_blocks):
        message[p, :BLK] = acc[p].astype(BF16)
        high, low = whole_parts(rows[p : p + 1])
        extra = jnp.where(line == 0, high, jnp.where(line == 1, low, 0.0))
        message[p, BLK:] = extra.astype(BF16)


def node_kernel(partials, weight, bias, cotangent, activations, message):
    parts = message.shape[0]
    chunk = BLK // parts
    total = jnp.sum(partials[...].astype(F32), axis=0)
    summed = total[:BLK]
    degree = 1.0 + total[BLK : BLK + 1] + total[BLK + 1 : BLK + 2]
    scale = jnp.sum(jnp.where(eye(BLK), lax.rsqrt(degree), 0.0), axis=1, keepdims=True)
    high, low = split(summed)
    high, low = high.astype(BF16), low.astype(BF16)
    product = jnp.dot(high, weight[...], preferred_element_type=F32)
    product += jnp.dot(low, weight[...], preferred_element_type=F32)
    pre = scale * product + bias[...]
    sigmoid = jax.nn.sigmoid(pre)
    activations[...] = (pre * sigmoid).astype(BF16)
    grad_pre = cotangent[...].astype(F32) * sigmoid * (1.0 + pre * (1.0 - sigmoid))
    back = (scale * grad_pre).astype(BF16)
    sent = lax.dot_general(weight[...], back, NT, preferred_element_type=F32).astype(BF16)
    grad = lax.dot_general(high, back, TN, preferred_element_type=F32)
    grad += lax.dot_general(low, back, TN, preferred_element_type=F32)
    extra = bias_rows(jnp.sum(grad_pre, axis=0, keepdims=True))
    for c in range(parts):
        piece = grad[c * chunk : (c + 1) * chunk]
        message[c, :BLK] = sent
        message[c, BLK : BLK + 2 * chunk] = jnp.concatenate(
            [piece[:, :BLK], piece[:, BLK:]], axis=0
        ).astype(BF16)
        message[c, BLK + 2 * chunk :] = extra


def bias_rows(value):
    line = lax.broadcasted_iota(jnp.int32, (16, BLK), 0)
    high, low = split(value)
    rows = [high[:, :BLK], high[:, BLK:], low[:, :BLK], low[:, BLK:]]
    result = jnp.zeros((16, BLK), F32)
    for i, row in enumerate(rows):
        result = jnp.where(line == i, row, result)
    return result.astype(BF16)


def bias_of(rows):
    return jnp.concatenate([rows[0:1] + rows[2:3], rows[1:2] + rows[3:4]], axis=1)


def backward_half(info, plan, tiles, message, sources, acc, start):
    half, row_blocks = acc.shape[0], message.shape[0]
    row_devices = 2 * half
    parity, diagonal = info[1], info[2]
    second_kind = row_blocks * row_devices
    lengths = 2 * second_kind + row_blocks
    for p in range(row_blocks):
        sources[p] = message[p, :BLK]
    sources[row_blocks] = jnp.zeros((BLK, BLK), BF16)
    acc[...] = jnp.zeros_like(acc)

    @pl.when(diagonal == 1)
    def _():
        shift = parity if start == 0 else 1 - parity
        for i in range(row_blocks // 2):
            p = 2 * i + shift
            acc[slot_of(parity * row_blocks + p, parity, half) - start] = sources[p].astype(F32)

    def pair(k, j):
        at = second_kind + (start + k) * row_blocks + 2 * j
        first, second = plan[at], plan[at + 1]
        left = jnp.concatenate([sources[first & MASK], sources[second & MASK]], axis=1)
        right = jnp.concatenate([tiles[first >> CODE], tiles[second >> CODE]], axis=0)
        return jnp.dot(left, right, preferred_element_type=F32)

    fixed = min(COL_PAIRS, row_blocks // 2)
    for k in range(half):
        total = acc[k]
        for j in range(fixed):
            total += pair(k, j)
        acc[k] = total

    @pl.when(plan[lengths + row_devices + 1] > 2 * fixed)
    def _():
        for k in range(half):

            def more(j, carry):
                acc[k] += pair(k, j)
                return carry

            lax.fori_loop(fixed, (plan[lengths + start + k] + 1) // 2, more, 0)


def backward_other_kernel(info, plan, tiles, message, other, sources, acc):
    half = acc.shape[0]
    backward_half(info, plan, tiles, message, sources, acc, half)
    for k in range(half):
        other[k * BLK : (k + 1) * BLK] = acc[k].astype(BF16)
    tail = jnp.sum(message[:, BLK:].astype(F32), axis=0)
    size = tail.shape[0] - 16
    high, low = split(tail[:size])
    at = half * BLK
    other[at : at + size] = high.astype(BF16)
    other[at + size : at + 2 * size] = low.astype(BF16)
    other[at + 2 * size :] = bias_rows(bias_of(tail[size:]))


def backward_own_kernel(info, plan, tiles, message, own, sources, acc):
    backward_half(info, plan, tiles, message, sources, acc, 0)
    own[...] = acc[...].astype(BF16)


def pair_kernel(partials, own, arrived, message):
    half = own.shape[0]
    tail = jnp.sum(partials[:, BLK:].astype(F32), axis=0)
    size = tail.shape[0] - 16
    at = half * BLK
    theirs = arrived[at:].astype(F32)
    chunk = (tail[:size] + theirs[:size] + theirs[size : 2 * size]).astype(BF16)
    extra = bias_rows(bias_of(tail[size:]) + bias_of(theirs[2 * size :]))
    for k in range(half):
        message[k, :BLK] = (
            own[k].astype(F32) + arrived[k * BLK : (k + 1) * BLK].astype(F32)
        ).astype(BF16)
        message[k, BLK : BLK + size] = chunk
        message[k, BLK + size :] = extra


def tail_kernel(message, chunks, grad_bias):
    tail = jnp.sum(message[:, BLK:].astype(F32), axis=0)
    chunk = (tail.shape[0] - 16) // 2
    piece = jnp.concatenate([tail[:chunk], tail[chunk : 2 * chunk]], axis=1)
    for c in range(chunks.shape[0]):
        chunks[c] = piece
    grad_bias[...] = bias_of(tail[2 * chunk :])


def last_kernel(info, message, scale, grad_inputs):
    total = jnp.sum(message[:, :BLK].astype(F32), axis=0)
    total = total * scale[pl.ds(info[3], 1), :]
    grad_inputs[...] = total.T.astype(BF16)


def per_device(node_inputs, weight, bias, edge_tiles, block_coords, block_counts, out_cotangent):
    row_devices = lax.axis_size("row")
    row_blocks = lax.axis_size("col")
    half = row_devices // 2
    slots = edge_tiles.shape[1]
    tiles = edge_tiles[0]
    coords = block_coords[0]
    row_index = lax.axis_index("row")
    col_index = lax.axis_index("col")
    diagonal = (col_index == row_index // (row_devices // row_blocks)).astype(jnp.int32)
    info = jnp.stack([block_counts[0, 0], row_index % 2, diagonal, row_index % 2 * half + row_index // 2])
    parities = [[2 * k + h for k in range(half)] for h in range(2)]
    partner = [(i, i ^ 1) for i in range(row_devices)]
    work = 2 * slots * BLK**3

    pieces = call(
        count_kernel,
        "count",
        (info, coords, tiles, node_inputs),
        [SMEM, SMEM, pl.BlockSpec(memory_space=pl.ANY), VMEM],
        struct((half, BLK + row_devices, BLK), BF16),
        [
            pltpu.VMEM((slots, BLK, BLK), BF16),
            pltpu.VMEM((row_devices, 16, BLK), F32),
            pltpu.SemaphoreType.DMA((PARTS,)),
        ],
        work // 128,
        56,
    )
    pieces = lax.all_to_all(pieces, "row", 0, 0, tiled=True, axis_index_groups=parities)
    entries = 2 * row_blocks * row_devices + row_blocks + row_devices + 2
    row_count, plan = call(
        plan_kernel,
        "plan",
        (info, coords, tiles),
        [SMEM, SMEM, VMEM],
        [struct((row_blocks, BLK), F32), struct((entries,), jnp.int32)],
        [pltpu.VMEM((row_blocks, 8, BLK), F32)],
        work // 16,
        out_specs=[VMEM, SMEM],
    )
    pieces, row_count = lax.optimization_barrier((pieces, row_count))
    pieces_other = lax.ppermute(pieces, "row", partner)
    message, scale = call(
        forward_kernel,
        "forward",
        (info, plan, tiles, pieces, pieces_other, row_count),
        [SMEM, SMEM] + [VMEM] * 4,
        [struct((row_blocks, BLK + 16, BLK), BF16), struct((row_devices, BLK), F32)],
        [pltpu.VMEM((row_devices + 1, BLK, BLK), BF16), pltpu.VMEM((row_blocks, BLK, BLK), F32)],
        work,
    )
    message = lax.all_to_all(message, "col", 0, 0, tiled=True)
    width = weight.shape[1]
    chunk = BLK // row_blocks
    activations, message = call(
        node_kernel,
        "node",
        (message, weight, bias.reshape(1, width), out_cotangent),
        [VMEM] * 4,
        [
            struct((BLK, width), BF16),
            struct((row_blocks, BLK + 2 * chunk + 16, BLK), BF16),
        ],
        (),
        8 * BLK * BLK * width,
    )
    message = lax.all_to_all(message, "col", 0, 0, tiled=True)
    scratch = [pltpu.VMEM((row_blocks + 1, BLK, BLK), BF16), pltpu.VMEM((half, BLK, BLK), F32)]
    other = call(
        backward_other_kernel,
        "backward_other",
        (info, plan, tiles, message),
        [SMEM, SMEM, VMEM, VMEM],
        struct((half * BLK + 4 * chunk + 16, BLK), BF16),
        scratch,
        work,
    )
    arrived = lax.ppermute(other, "row", partner)
    own = call(
        backward_own_kernel,
        "backward_own",
        (info, plan, tiles, message),
        [SMEM, SMEM, VMEM, VMEM],
        struct((half, BLK, BLK), BF16),
        scratch,
        work,
    )
    message = call(
        pair_kernel,
        "pair",
        (message, own, arrived),
        [VMEM] * 3,
        struct((half, BLK + 2 * chunk + 16, BLK), BF16),
    )
    message = lax.all_to_all(message, "row", 0, 0, tiled=True, axis_index_groups=parities)
    chunks, grad_bias = call(
        tail_kernel,
        "tail",
        (message,),
        [VMEM],
        [struct((row_blocks, chunk, width), F32), struct((1, width), F32)],
    )
    grad_weight = lax.all_to_all(chunks, "col", 0, 0, tiled=True)
    grad_inputs = call(
        last_kernel, "last", (info, message, scale), [SMEM, VMEM, VMEM], struct((BLK, BLK), BF16)
    )
    return activations, grad_inputs, grad_weight.reshape(BLK, width), grad_bias.reshape(width)


def solution(mesh):
    in_specs = (
        P(("col", "row"), None),
        P(),
        P(),
        P("row", "col", None, None),
        P("row", "col", None),
        P("row", "col"),
        P(("row", "col"), None),
    )
    out_specs = (P(("row", "col"), None), P(("col", "row"), None), P(), P())
    return jax.shard_map(
        per_device, mesh=mesh, in_specs=in_specs, out_specs=out_specs, check_vma=False
    )
```

time: 160 us -> 145 us (0.906)
  blocking collectives: 102 us -> 82.1 us
  Pallas kernels: 10 us -> 17.4 us
  waiting for transfers between devices: 25 us -> 20.7 us
  local copies, waits for them, and re-layouts: 3.18 us -> 4.8 us
    all_to_all x1 -> x0, blocking collectives: 15.3 us -> none  [per_device(): lax.all_to_all(grads, 'row', 0, 0, tiled=True, axis_index_groups=parities)]
    pallas_call x9, Pallas kernels: 10 us -> 17.4 us  [call(): pl.pallas_call(kernel, out_shape=outs, in_specs=specs, out_specs=out_spec...]
    all_to_all x1 -> x2, starting transfers between devices: 6.91 us -> 13 us  [the longest x1 8.78 us: per_device(): lax.all_to_all(pieces, 'row', 0, 0, tiled=True, axis_index_groups=parities)]
    ppermute x2 -> x1, starting transfers between devices: 7.35 us -> 2.04 us  [per_device(): pieces_other = lax.ppermute(pieces, 'row', partner)]
    all_to_all x1, blocking collectives: 28.6 us -> 25.1 us  [per_device(): lax.all_to_all(message, 'row', 0, 0, tiled=True, axis_index_groups=parities)]
    all_to_all x1 -> x2, waiting for transfers between devices: 20.8 us -> 18.5 us  [the longest x1 12.5 us: per_device(): lax.all_to_all(pieces, 'row', 0, 0, tiled=True, axis_index_groups=parities)]
    unnamed x13 -> x22, local copies, waits for them, and re-layouts: 2.62 us -> 4.8 us
  transfers between devices with their start and end apart: 4 -> 4, of which waited for: 4 -> 4; matrix products, arithmetic and copies ran while one was open for 0% -> 0% of each run, Pallas kernels for 0% -> 5%
where the time goes in v2:
time: 145 us; the launch traced here: 144 us
  blocking collectives  82.1 us (57%)
  waiting for transfers between devices  20.7 us (14%)
  Pallas kernels  17.4 us (12%)
  starting transfers between devices  16.9 us (12%)
  local copies, waits for them, and re-layouts  4.8 us (3%)
  between operations  1.58 us (1%)
    all_to_all x2, blocking collectives, per_device(): message = lax.all_to_all(message, 'col', 0, 0, tiled=True)  56.9 us
    all_to_all x1, blocking collectives, per_device(): lax.all_to_all(message, 'row', 0, 0, tiled=True, axis_index_groups=parities)  25.1 us
    pallas_call x9, Pallas kernels, call(): pl.pallas_call(kernel, out_shape=outs, in_specs=specs, out_specs=out_spec...  17.4 us
    all_to_all x1, waiting for transfers between devices, per_device(): lax.all_to_all(pieces, 'row', 0, 0, tiled=True, axis_index_groups=parities)  12.5 us
    all_to_all x1, starting transfers between devices, per_device(): lax.all_to_all(pieces, 'row', 0, 0, tiled=True, axis_index_groups=parities)  8.78 us
    all_to_all x1, waiting for transfers between devices, per_device(): grad_weight = lax.all_to_all(chunks, 'col', 0, 0, tiled=True)  6.01 us
    unnamed x22, local copies, waits for them, and re-layouts  4.8 us
    all_to_all x1, starting transfers between devices, per_device(): grad_weight = lax.all_to_all(chunks, 'col', 0, 0, tiled=True)  4.19 us
  transfers between devices with their start and end apart: 4, of which 4 were waited for; matrix products, arithmetic and copies ran while one was open for 0% of the time, Pallas kernels for 5%

profile of v2, /device:TPU:8, one launch (start us, length us, event | category | flops | bytes accessed | tf_op | source)
XLA Modules:
  0.0 144.1 jit_solution(9042370734545615283)
XLA Ops:
  0.6 0.0 copy-start
  1.5 1.4 %copy.11 = s32[1,88,2]{2,1,0:T(8,128)} copy(s32[1,88,2]{1,2,0:T(2,128)} %param.11) | data formatting | bytes 1408 | tf_op args[4]
  2.9 0.7 pad_add_fusion.info
  3.6 0.0 copy-start.4
  3.6 4.1 %count.1 = bf16[16,160,128]{2,1,0:T(8,128)(2,1)} custom-call(s32[4]{0:T(128)} %pad_add_fusion.info, s32[88,2]{1,0:T(8,128)} %bitcast.15, bf16[88,128,128]{2,1,0:T(8,128)(2,1)} %bitcast.10, bf16[128,128]{1,0:T(8,128)(2,1)} %x.1), custom_call_target="tpu_custom_call" | custom-call | flops 2883584 | bytes 3572432 | tf_op jit(solution)/shard_map/count/pallas_call | solution.py:31
  7.7 8.8 %all-to-all-start = ((bf16[16,160,128]{2,1,0:T(8,128)(2,1)}), bf16[16,160,128]{2,1,0:T(8,128)(2,1)S(1)}, u32[]{:S(2)}, u32[]{:S(2)}) async-start(bf16[16,160,128]{2,1,0:T(8,128)(2,1)} %count.1), calls=%async_computation | async-start | bytes 1310720 | tf_op jit(solution)/shard_map/all_to_all | solution.py:373
  16.5 0.0 copy-done
  16.5 0.0 copy-done.4
  16.5 0.0 copy-start.1
  16.5 0.8 copy-done.1
  17.3 0.0 copy-start.9
  17.3 3.6 %plan.1 = (f32[16,128]{1,0:T(8,128)S(1)}, s32[1074]{0:T(1024)S(1)}) custom-call(s32[4]{0:T(128)S(1)} %copy-done.4, s32[88,2]{1,0:T(8,128)S(1)} %bitcast.16, bf16[88,128,128]{2,1,0:T(8,128)(2,1)S(1)} %bitcast.11), custom_call_target="tpu_custom_call" | custom-call | flops 23068672 | bytes 2896792 | tf_op jit(solution)/shard_map/plan/pallas_call | solution.py:31
  20.9 0.0 copy-start.7
  20.9 0.6 copy-done.7
  21.5 12.5 %all-to-all-done.own = bf16[16,160,128]{2,1,0:T(8,128)(2,1)S(1)} async-done(((bf16[16,160,128]{2,1,0:T(8,128)(2,1)}), bf16[16,160,128]{2,1,0:T(8,128)(2,1)S(1)}, u32[]{:S(2)}, u32[]{:S(2)}) %all-to-all-start) | async-done | bytes 655392 | tf_op jit(solution)/shard_map/all_to_all | solution.py:373
  34.0 0.0 copy-start.2
  34.0 0.0 copy-start.3
  34.0 2.0 %collective-permute-start = (bf16[16,160,128]{2,1,0:T(8,128)(2,1)S(1)}, bf16[16,160,128]{2,1,0:T(8,128)(2,1)S(1)}, u32[]{:S(2)}, u32[]{:S(2)}) collective-permute-start(bf16[16,160,128]{2,1,0:T(8,128)(2,1)S(1)} %all-to-all-done.own), channel_id=1, source_target_pairs={{0,16},{16,0},{32,48},{48,32},{64,80},{80,64},{96,112},{112,96},{1... | collective-permute-start | bytes 1966088 | tf_op jit(solution)/shard_map/ppermute | solution.py:386
  36.1 2.1 %collective-permute-done.other = bf16[16,160,128]{2,1,0:T(8,128)(2,1)S(1)} collective-permute-done((bf16[16,160,128]{2,1,0:T(8,128)(2,1)S(1)}, bf16[16,160,128]{2,1,0:T(8,128)(2,1)S(1)}, u32[]{:S(2)}, u32[]{:S(2)}) %collective-permute-start) | collective-permute-done | bytes 655392 | tf_op jit(solution)/shard_map/ppermute | solution.py:386
  38.2 0.0 copy-start.8
  38.2 0.7 copy-done.8
  38.9 3.0 %forward.1 = (bf16[16,144,128]{2,1,0:T(8,128)(2,1)S(1)}, f32[32,128]{1,0:T(8,128)S(1)}) custom-call(s32[4]{0:T(128)S(1)} %copy-done.4, s32[1074]{0:T(1024)S(1)} %get-tuple-element.14.plan, bf16[88,128,128]{2,1,0:T(8,128)(2,1)S(1)} %bitcast.12, bf16[16,160,128]{2,1,0:T(8,128)(2,1)S(1)} %all-to-all-done.own, ...), custom_call_target="tpu_custom_call" | custom-call | flops 369098752 | bytes 4813016 | tf_op jit(solution)/shard_map/forward/pallas_call | solution.py:31
  41.9 0.0 copy-start.5
  41.9 0.6 copy-done.5
  42.5 33.7 %all_to_all.25.partials = bf16[16,144,128]{2,1,0:T(8,128)(2,1)S(1)} all-to-all(bf16[16,144,128]{2,1,0:T(8,128)(2,1)S(1)} %get-tuple-element.18), channel_id=1, replica_groups=mesh['row'=32,'col'=16] {'col'}, dimensions={0} | all-to-all | bytes 1179648 | tf_op jit(solution)/shard_map/all_to_all | solution.py:396
  76.2 0.0 copy-done.9
  76.2 0.0 copy-done.2
  76.2 0.0 copy-done.3
  76.2 0.9 node.1
  77.1 23.3 %all_to_all.26.message.partials = bf16[16,160,128]{2,1,0:T(8,128)(2,1)S(1)} all-to-all(bf16[16,160,128]{2,1,0:T(8,128)(2,1)S(1)} %get-tuple-element.20), channel_id=1, replica_groups=mesh['row'=32,'col'=16] {'col'}, dimensions={0} | all-to-all | bytes 1310720 | tf_op jit(solution)/shard_map/all_to_all | solution.py:411
  100.3 1.8 %backward_other.1 = bf16[2096,128]{1,0:T(8,128)(2,1)S(1)} custom-call(s32[4]{0:T(128)S(1)} %copy-done.4, s32[1074]{0:T(1024)S(1)} %get-tuple-element.14.plan, bf16[88,128,128]{2,1,0:T(8,128)(2,1)S(1)} %bitcast.13, bf16[16,160,128]{2,1,0:T(8,128)(2,1)S(1)} %all_to_all.26.message.partials), custom_call_target="tpu_custom_call" | custom-call | flops 369098752 | bytes 4079832 | tf_op jit(solution)/shard_map/backward_other/pallas_call | solution.py:31
  102.1 1.9 %collective-permute-start.1 = (bf16[2096,128]{1,0:T(8,128)(2,1)S(1)}, bf16[2096,128]{1,0:T(8,128)(2,1)S(1)}, u32[]{:S(2)}, u32[]{:S(2)}) collective-permute-start(bf16[2096,128]{1,0:T(8,128)(2,1)S(1)} %backward_other.1), channel_id=1, source_target_pairs={{0,16},{16,0},{32,48},{48,32},{64,80},{80,64},{96,112},{112,96},{1... | collective-permute-start | bytes 1609736 | tf_op jit(solution)/shard_map/ppermute | solution.py:422
  104.0 1.8 %backward_own.1.own = bf16[16,128,128]{2,1,0:T(8,128)(2,1)S(1)} custom-call(s32[4]{0:T(128)S(1)} %copy-done.4, s32[1074]{0:T(1024)S(1)} %get-tuple-element.14.plan, bf16[88,128,128]{2,1,0:T(8,128)(2,1)S(1)} %bitcast.14, bf16[16,160,128]{2,1,0:T(8,128)(2,1)S(1)} %all_to_all.26.message.partials), custom_call_target="tpu_custom_call" | custom-call | flops 369098752 | bytes 4067544 | tf_op jit(solution)/shard_map/backward_own/pallas_call | solution.py:31
  105.8 0.0 copy-start.6
  105.8 0.1 collective-permute-done.1.arrived
  105.9 0.2 pair.1
  106.1 25.1 %all_to_all.27.message = bf16[16,160,128]{2,1,0:T(8,128)(2,1)S(1)} all-to-all(bf16[16,160,128]{2,1,0:T(8,128)(2,1)S(1)} %pair.1), channel_id=1, replica_groups={{0,32,64,96,128,160,192,224,256,288,320,352,384,416,448,480},{16,48,80,..., dimensions={0} | all-to-all | bytes 1310720 | tf_op jit(solution)/shard_map/all_to_all | solution.py:439
  131.2 0.7 tail.1
  131.9 4.2 %all-to-all-start.4 = ((f32[16,8,256]{2,1,0:T(8,128)}), f32[16,8,256]{2,1,0:T(8,128)S(1)}, u32[]{:S(2)}, u32[]{:S(2)}) async-start(f32[16,8,256]{2,1,0:T(8,128)} %get-tuple-element.22), calls=%async_computation.4 | async-start | bytes 262144 | tf_op jit(solution)/shard_map/all_to_all | solution.py:447
  136.1 0.0 copy-done.6
  136.1 1.3 last.1
  137.4 6.0 %all-to-all-done.4 = f32[16,8,256]{2,1,0:T(8,128)S(1)} async-done(((f32[16,8,256]{2,1,0:T(8,128)}), f32[16,8,256]{2,1,0:T(8,128)S(1)}, u32[]{:S(2)}, u32[]{:S(2)}) %all-to-all-start.4) | async-done | bytes 131104 | tf_op jit(solution)/shard_map/all_to_all | solution.py:447
  143.4 0.7 copy.14
Async XLA Ops:
  0.6 15.9 %copy-start = (bf16[1,88,128,128]{3,2,1,0:T(8,128)(2,1)S(1)}, bf16[1,88,128,128]{3,2,1,0:T(8,128)(2,1)}, u32[]{:S(2)}) copy-start(bf16[1,88,128,128]{3,2,1,0:T(8,128)(2,1)} %param.10) | copy-start | bytes 8650756
  3.6 13.0 %copy-start.4 = (s32[4]{0:T(128)S(1)}, s32[4]{0:T(128)}, u32[]{:S(2)}) copy-start(s32[4]{0:T(128)} %pad_add_fusion.info) | copy-start | bytes 52
  7.7 26.3 %all-to-all-start = ((bf16[16,160,128]{2,1,0:T(8,128)(2,1)}), bf16[16,160,128]{2,1,0:T(8,128)(2,1)S(1)}, u32[]{:S(2)}, u32[]{:S(2)}) async-start(bf16[16,160,128]{2,1,0:T(8,128)(2,1)} %count.1), calls=%async_computation | async-start | bytes 1310720 | tf_op jit(solution)/shard_map/all_to_all | solution.py:373
  16.5 0.8 copy-start.1
  17.3 58.8 %copy-start.9 = (f32[256]{0:T(256)S(1)}, f32[256]{0:T(256)}, u32[]{:S(2)}) copy-start(f32[256]{0:T(256)} %param.9) | copy-start | bytes 3076
  20.9 0.6 copy-start.7
  34.0 42.1 %copy-start.2 = (bf16[128,256]{1,0:T(8,128)(2,1)S(1)}, bf16[128,256]{1,0:T(8,128)(2,1)}, u32[]{:S(2)}) copy-start(bf16[128,256]{1,0:T(8,128)(2,1)} %weight.1) | copy-start | bytes 196612
  34.0 42.1 %copy-start.3 = (bf16[128,256]{1,0:T(8,128)(2,1)S(1)}, bf16[128,256]{1,0:T(8,128)(2,1)}, u32[]{:S(2)}) copy-start(bf16[128,256]{1,0:T(8,128)(2,1)} %cotangent.1) | copy-start | bytes 196612
  34.0 4.1 %collective-permute-start = (bf16[16,160,128]{2,1,0:T(8,128)(2,1)S(1)}, bf16[16,160,128]{2,1,0:T(8,128)(2,1)S(1)}, u32[]{:S(2)}, u32[]{:S(2)}) collective-permute-start(bf16[16,160,128]{2,1,0:T(8,128)(2,1)S(1)} %all-to-all-done.own), channel_id=1, source_target_pairs={{0,16},{16,0},{32,48},{48,32},{64,80},{80,64},{96,112},{112,96},{1... | collective-permute-start | bytes 1966088 | tf_op jit(solution)/shard_map/ppermute | solution.py:386
  38.2 0.7 copy-start.8
  41.9 0.6 copy-start.5
  102.1 3.8 %collective-permute-start.1 = (bf16[2096,128]{1,0:T(8,128)(2,1)S(1)}, bf16[2096,128]{1,0:T(8,128)(2,1)S(1)}, u32[]{:S(2)}, u32[]{:S(2)}) collective-permute-start(bf16[2096,128]{1,0:T(8,128)(2,1)S(1)} %backward_other.1), channel_id=1, source_target_pairs={{0,16},{16,0},{32,48},{48,32},{64,80},{80,64},{96,112},{112,96},{1... | collective-permute-start | bytes 1609736 | tf_op jit(solution)/shard_map/ppermute | solution.py:422
  105.8 30.3 %copy-start.6 = (f32[32,128]{1,0:T(8,128)S(1)}, f32[32,128]{1,0:T(8,128)}, u32[]{:S(2)}) copy-start(f32[32,128]{1,0:T(8,128)} %copy-done.5) | copy-start | bytes 49156
  131.9 11.5 %all-to-all-start.4 = ((f32[16,8,256]{2,1,0:T(8,128)}), f32[16,8,256]{2,1,0:T(8,128)S(1)}, u32[]{:S(2)}, u32[]{:S(2)}) async-start(f32[16,8,256]{2,1,0:T(8,128)} %get-tuple-element.22), calls=%async_computation.4 | async-start | bytes 262144 | tf_op jit(solution)/shard_map/all_to_all | solution.py:447

commit v3 on v2

--- a/solution.py
+++ b/solution.py
@@ -8,6 +8,7 @@
 
 BLK = 128
 GROUP = 4
+TAIL = 8
 UNROLL = 2
 PARTS = 4
 CODE = 6
@@ -18,6 +19,7 @@
 BF16 = jnp.bfloat16
 VMEM = pl.BlockSpec(memory_space=pltpu.VMEM)
 SMEM = pl.BlockSpec(memory_space=pltpu.SMEM)
+ANY = pl.BlockSpec(memory_space=pl.ANY)
 NT = (((1,), (1,)), ((), ()))
 TN = (((0,), (0,)), ((), ()))
 
@@ -60,14 +62,21 @@
     return ((q & 1) ^ parity) * half + (q >> 1)
 
 
+def place(row_devices, row_blocks):
+    row, col = lax.axis_index("row"), lax.axis_index("col")
+    diagonal = col == row // (row_devices // row_blocks)
+    return row & 1, row >> 1, diagonal
+
+
 def eye(n):
     return lax.broadcasted_iota(jnp.int32, (n, n), 0) == lax.broadcasted_iota(jnp.int32, (n, n), 1)
 
 
-def count_kernel(info, coords, tiles, x, message, held, col_acc, arrivals):
+def count_kernel(live_slots, coords, tiles, x, message, held, col_acc, arrivals):
     col_acc[...] = jnp.zeros_like(col_acc)
-    count, parity = info[0], info[1]
     half = col_acc.shape[0] // 2
+    count = live_slots[0, 0]
+    parity = lax.axis_index("row") & 1
     part = held.shape[0] // PARTS
     copies = [
         pltpu.make_async_copy(
@@ -83,7 +92,7 @@
             s = g * UNROLL + u
             live = jnp.where(s < count, 1.0, 0.0).astype(F32)
             column = jnp.sum(held[s].reshape(BLK // 16, 16, BLK), axis=0)
-            col_acc[slot_of(coords[s, 1], parity, half)] += column.astype(F32) * live
+            col_acc[slot_of(coords[1, s], parity, half)] += column.astype(F32) * live
         return carry
 
     for i, copy in enumerate(copies):
@@ -100,14 +109,15 @@
         message[k, BLK:] = total
 
 
-def plan_kernel(info, coords, tiles, rows, plan, row_acc):
+def plan_kernel(live_slots, coords, tiles, rows, plan, row_acc):
     row_blocks = rows.shape[0]
     row_devices = (plan.shape[0] - 2 - row_blocks) // (2 * row_blocks + 1)
     half = row_devices // 2
     second = row_blocks * row_devices
     lengths = 2 * second
     longest = lengths + row_blocks + row_devices
-    count, parity = info[0], info[1]
+    count = live_slots[0, 0]
+    parity = lax.axis_index("row") & 1
 
     def blank(i, carry):
         plan[i] = row_devices
@@ -119,8 +129,8 @@
         plan[lengths + i] = 0
 
     def enter(s, carry):
-        p = coords[s, 0]
-        slot = slot_of(coords[s, 1], parity, half)
+        p = coords[0, s]
+        slot = slot_of(coords[1, s], parity, half)
         at_row, at_col = lengths + p, lengths + row_blocks + slot
         n_row, n_col = plan[at_row], plan[at_col]
         plan[p * row_devices + n_row] = (s << CODE) + slot
@@ -141,7 +151,7 @@
             s = g * GROUP + u
             live = jnp.where(s < count, 1.0, 0.0).astype(F32)
             line = lax.dot_general(ones, tiles[s], NT, preferred_element_type=F32)
-            row_acc[coords[s, 0]] += line * live
+            row_acc[coords[0, s]] += line * live
         return carry
 
     lax.fori_loop(0, (count + GROUP - 1) // GROUP, group, 0)
@@ -153,12 +163,18 @@
     return high, total - high
 
 
-def forward_kernel(info, plan, tiles, own, other, rows, message, scale, features, acc):
+def forward_kernel(
+    plan, tiles, own, other, rows_in, message, scale_out, features, acc, rows, scale, moved
+):
     half, row_blocks = own.shape[0], message.shape[0]
-    parity, diagonal = info[1], info[2]
+    parity, _, diagonal = place(2 * half, row_blocks)
+    arriving = pltpu.make_async_copy(rows_in, rows, moved.at[0])
+    arriving.start()
     degree = 1.0 + jnp.sum(own[:, BLK:].astype(F32) + other[:, BLK:].astype(F32), axis=0)
     factor = lax.rsqrt(degree)
     scale[...] = factor
+    leaving = pltpu.make_async_copy(scale, scale_out, moved.at[1])
+    leaving.start()
     turned = lax.dot_general(
         eye(BLK).astype(F32), factor, NT, precision=lax.Precision.HIGHEST, preferred_element_type=F32
     )
@@ -182,7 +198,7 @@
     fixed = min(ROW_PAIRS, half)
     for p in range(row_blocks):
         same = features[slot_of(parity * row_blocks + p, parity, half)].astype(F32)
-        total = jnp.where(diagonal == 1, same, 0.0)
+        total = jnp.where(diagonal, same, 0.0)
         for j in range(fixed):
             total += pair(p, j)
         acc[p] = total
@@ -197,12 +213,14 @@
 
             lax.fori_loop(fixed, (plan[lengths + p] + 1) // 2, more, 0)
 
-    line = lax.broadcasted_iota(jnp.int32, (16, BLK), 0)
+    arriving.wait()
+    line = lax.broadcasted_iota(jnp.int32, (TAIL, BLK), 0)
     for p in range(row_blocks):
         message[p, :BLK] = acc[p].astype(BF16)
         high, low = whole_parts(rows[p : p + 1])
         extra = jnp.where(line == 0, high, jnp.where(line == 1, low, 0.0))
         message[p, BLK:] = extra.astype(BF16)
+    leaving.wait()
 
 
 def node_kernel(partials, weight, bias, cotangent, activations, message):
@@ -235,10 +253,10 @@
 
 
 def bias_rows(value):
-    line = lax.broadcasted_iota(jnp.int32, (16, BLK), 0)
+    line = lax.broadcasted_iota(jnp.int32, (TAIL, BLK), 0)
     high, low = split(value)
     rows = [high[:, :BLK], high[:, BLK:], low[:, :BLK], low[:, BLK:]]
-    result = jnp.zeros((16, BLK), F32)
+    result = jnp.zeros((TAIL, BLK), F32)
     for i, row in enumerate(rows):
         result = jnp.where(line == i, row, result)
     return result.astype(BF16)
@@ -248,10 +266,10 @@
     return jnp.concatenate([rows[0:1] + rows[2:3], rows[1:2] + rows[3:4]], axis=1)
 
 
-def backward_half(info, plan, tiles, message, sources, acc, start):
+def backward_half(plan, tiles, message, sources, acc, start):
     half, row_blocks = acc.shape[0], message.shape[0]
     row_devices = 2 * half
-    parity, diagonal = info[1], info[2]
+    parity, _, diagonal = place(row_devices, row_blocks)
     second_kind = row_blocks * row_devices
     lengths = 2 * second_kind + row_blocks
     for p in range(row_blocks):
@@ -259,7 +277,7 @@
     sources[row_blocks] = jnp.zeros((BLK, BLK), BF16)
     acc[...] = jnp.zeros_like(acc)
 
-    @pl.when(diagonal == 1)
+    @pl.when(diagonal)
     def _():
         shift = parity if start == 0 else 1 - parity
         for i in range(row_blocks // 2):
@@ -291,33 +309,34 @@
             lax.fori_loop(fixed, (plan[lengths + start + k] + 1) // 2, more, 0)
 
 
-def backward_other_kernel(info, plan, tiles, message, other, sources, acc):
+def backward_other_kernel(plan, tiles, message, other, sources, acc):
     half = acc.shape[0]
-    backward_half(info, plan, tiles, message, sources, acc, half)
+    backward_half(plan, tiles, message, sources, acc, half)
     for k in range(half):
         other[k * BLK : (k + 1) * BLK] = acc[k].astype(BF16)
     tail = jnp.sum(message[:, BLK:].astype(F32), axis=0)
-    size = tail.shape[0] - 16
+    size = tail.shape[0] - TAIL
     high, low = split(tail[:size])
     at = half * BLK
     other[at : at + size] = high.astype(BF16)
     other[at + size : at + 2 * size] = low.astype(BF16)
-    other[at + 2 * size :] = bias_rows(bias_of(tail[size:]))
-
-
-def backward_own_kernel(info, plan, tiles, message, own, sources, acc):
-    backward_half(info, plan, tiles, message, sources, acc, 0)
+    other[at + 2 * size : at + 2 * size + TAIL] = bias_rows(bias_of(tail[size:]))
+    other[at + 2 * size + TAIL :] = jnp.zeros((16 - TAIL, BLK), BF16)
+
+
+def backward_own_kernel(plan, tiles, message, own, sources, acc):
+    backward_half(plan, tiles, message, sources, acc, 0)
     own[...] = acc[...].astype(BF16)
 
 
 def pair_kernel(partials, own, arrived, message):
     half = own.shape[0]
     tail = jnp.sum(partials[:, BLK:].astype(F32), axis=0)
-    size = tail.shape[0] - 16
+    size = tail.shape[0] - TAIL
     at = half * BLK
     theirs = arrived[at:].astype(F32)
     chunk = (tail[:size] + theirs[:size] + theirs[size : 2 * size]).astype(BF16)
-    extra = bias_rows(bias_of(tail[size:]) + bias_of(theirs[2 * size :]))
+    extra = bias_rows(bias_of(tail[size:]) + bias_of(theirs[2 * size : 2 * size + TAIL]))
     for k in range(half):
         message[k, :BLK] = (
             own[k].astype(F32) + arrived[k * BLK : (k + 1) * BLK].astype(F32)
@@ -328,16 +347,17 @@
 
 def tail_kernel(message, chunks, grad_bias):
     tail = jnp.sum(message[:, BLK:].astype(F32), axis=0)
-    chunk = (tail.shape[0] - 16) // 2
+    chunk = (tail.shape[0] - TAIL) // 2
     piece = jnp.concatenate([tail[:chunk], tail[chunk : 2 * chunk]], axis=1)
     for c in range(chunks.shape[0]):
         chunks[c] = piece
     grad_bias[...] = bias_of(tail[2 * chunk :])
 
 
-def last_kernel(info, message, scale, grad_inputs):
+def last_kernel(message, scale, grad_inputs):
+    parity, chip, _ = place(scale.shape[0], scale.shape[0])
     total = jnp.sum(message[:, :BLK].astype(F32), axis=0)
-    total = total * scale[pl.ds(info[3], 1), :]
+    total = total * scale[pl.ds(parity * message.shape[0] + chip, 1), :]
     grad_inputs[...] = total.T.astype(BF16)
 
 
@@ -347,11 +367,7 @@
     half = row_devices // 2
     slots = edge_tiles.shape[1]
     tiles = edge_tiles[0]
-    coords = block_coords[0]
-    row_index = lax.axis_index("row")
-    col_index = lax.axis_index("col")
-    diagonal = (col_index == row_index // (row_devices // row_blocks)).astype(jnp.int32)
-    info = jnp.stack([block_counts[0, 0], row_index % 2, diagonal, row_index % 2 * half + row_index // 2])
+    coords = block_coords[0].T
     parities = [[2 * k + h for k in range(half)] for h in range(2)]
     partner = [(i, i ^ 1) for i in range(row_devices)]
     work = 2 * slots * BLK**3
@@ -359,8 +375,8 @@
     pieces = call(
         count_kernel,
         "count",
-        (info, coords, tiles, node_inputs),
-        [SMEM, SMEM, pl.BlockSpec(memory_space=pl.ANY), VMEM],
+        (block_counts, coords, tiles, node_inputs),
+        [SMEM, SMEM, ANY, VMEM],
         struct((half, BLK + row_devices, BLK), BF16),
         [
             pltpu.VMEM((slots, BLK, BLK), BF16),
@@ -368,14 +384,14 @@
             pltpu.SemaphoreType.DMA((PARTS,)),
         ],
         work // 128,
-        56,
+        61,
     )
     pieces = lax.all_to_all(pieces, "row", 0, 0, tiled=True, axis_index_groups=parities)
     entries = 2 * row_blocks * row_devices + row_blocks + row_devices + 2
     row_count, plan = call(
         plan_kernel,
         "plan",
-        (info, coords, tiles),
+        (block_counts, coords, tiles),
         [SMEM, SMEM, VMEM],
         [struct((row_blocks, BLK), F32), struct((entries,), jnp.int32)],
         [pltpu.VMEM((row_blocks, 8, BLK), F32)],
@@ -387,11 +403,18 @@
     message, scale = call(
         forward_kernel,
         "forward",
-        (info, plan, tiles, pieces, pieces_other, row_count),
-        [SMEM, SMEM] + [VMEM] * 4,
-        [struct((row_blocks, BLK + 16, BLK), BF16), struct((row_devices, BLK), F32)],
-        [pltpu.VMEM((row_devices + 1, BLK, BLK), BF16), pltpu.VMEM((row_blocks, BLK, BLK), F32)],
+        (plan, tiles, pieces, pieces_other, row_count),
+        [SMEM] + [VMEM] * 3 + [ANY],
+        [struct((row_blocks, BLK + TAIL, BLK), BF16), struct((row_devices, BLK), F32)],
+        [
+            pltpu.VMEM((row_devices + 1, BLK, BLK), BF16),
+            pltpu.VMEM((row_blocks, BLK, BLK), F32),
+            pltpu.VMEM((row_blocks, BLK), F32),
+            pltpu.VMEM((row_devices, BLK), F32),
+            pltpu.SemaphoreType.DMA((2,)),
+        ],
         work,
+        out_specs=[VMEM, ANY],
     )
     message = lax.all_to_all(message, "col", 0, 0, tiled=True)
     width = weight.shape[1]
@@ -403,7 +426,7 @@
         [VMEM] * 4,
         [
             struct((BLK, width), BF16),
-            struct((row_blocks, BLK + 2 * chunk + 16, BLK), BF16),
+            struct((row_blocks, BLK + 2 * chunk + TAIL, BLK), BF16),
         ],
         (),
         8 * BLK * BLK * width,
@@ -413,8 +436,8 @@
     other = call(
         backward_other_kernel,
         "backward_other",
-        (info, plan, tiles, message),
-        [SMEM, SMEM, VMEM, VMEM],
+        (plan, tiles, message),
+        [SMEM, VMEM, VMEM],
         struct((half * BLK + 4 * chunk + 16, BLK), BF16),
         scratch,
         work,
@@ -423,8 +446,8 @@
     own = call(
         backward_own_kernel,
         "backward_own",
-        (info, plan, tiles, message),
-        [SMEM, SMEM, VMEM, VMEM],
+        (plan, tiles, message),
+        [SMEM, VMEM, VMEM],
         struct((half, BLK, BLK), BF16),
         scratch,
         work,
@@ -434,7 +457,7 @@
         "pair",
         (message, own, arrived),
         [VMEM] * 3,
-        struct((half, BLK + 2 * chunk + 16, BLK), BF16),
+        struct((half, BLK + 2 * chunk + TAIL, BLK), BF16),
     )
     message = lax.all_to_all(message, "row", 0, 0, tiled=True, axis_index_groups=parities)
     chunks, grad_bias = call(
@@ -446,7 +469,7 @@
     )
     grad_weight = lax.all_to_all(chunks, "col", 0, 0, tiled=True)
     grad_inputs = call(
-        last_kernel, "last", (info, message, scale), [SMEM, VMEM, VMEM], struct((BLK, BLK), BF16)
+        last_kernel, "last", (message, scale), [VMEM, VMEM], struct((BLK, BLK), BF16)
     )
     return activations, grad_inputs, grad_weight.reshape(BLK, width), grad_bias.reshape(width)
 

time: 145 us -> 140 us (0.966)
  local copies, waits for them, and re-layouts: 4.8 us -> 0.68 us
  waiting for transfers between devices: 20.7 us -> 23.8 us
  blocking collectives: 82.1 us -> 80.4 us
    unnamed x22 -> x11, local copies, waits for them, and re-layouts: 4.8 us -> 0.68 us
    all_to_all x1, waiting for transfers between devices: 12.5 us -> 14.6 us  [per_device(): lax.all_to_all(pieces, 'row', 0, 0, tiled=True, axis_index_groups=parities)]
    all_to_all x2, blocking collectives: 56.9 us -> 55.3 us  [per_device(): message = lax.all_to_all(message, 'col', 0, 0, tiled=True)]
  transfers between devices with their start and end apart: 4 -> 4, of which waited for: 4 -> 4; matrix products, arithmetic and copies ran while one was open for 0% -> 0% of each run, Pallas kernels for 5% -> 4%
where the time goes in v3:
time: 140 us; the launch traced here: 139 us
  blocking collectives  80.4 us (57%)
  waiting for transfers between devices  23.8 us (17%)
  starting transfers between devices  16.9 us (12%)
  Pallas kernels  16.1 us (12%)
  between operations  1.56 us (1%)
    all_to_all x2, blocking collectives, per_device(): message = lax.all_to_all(message, 'col', 0, 0, tiled=True)  55.3 us
    all_to_all x1, blocking collectives, per_device(): lax.all_to_all(message, 'row', 0, 0, tiled=True, axis_index_groups=parities)  25 us
    pallas_call x9, Pallas kernels, call(): pl.pallas_call(kernel, out_shape=outs, in_specs=specs, out_specs=out_spec...  16.1 us
    all_to_all x1, waiting for transfers between devices, per_device(): lax.all_to_all(pieces, 'row', 0, 0, tiled=True, axis_index_groups=parities)  14.6 us
    all_to_all x1, starting transfers between devices, per_device(): lax.all_to_all(pieces, 'row', 0, 0, tiled=True, axis_index_groups=parities)  9.03 us
    all_to_all x1, waiting for transfers between devices, per_device(): grad_weight = lax.all_to_all(chunks, 'col', 0, 0, tiled=True)  6.79 us
    all_to_all x1, starting transfers between devices, per_device(): grad_weight = lax.all_to_all(chunks, 'col', 0, 0, tiled=True)  4.02 us
  transfers between devices with their start and end apart: 4, of which 4 were waited for; matrix products, arithmetic and copies ran while one was open for 0% of the time, Pallas kernels for 4%

profile of v3, /device:TPU:8, one launch (start us, length us, event | category | flops | bytes accessed | tf_op | source)
XLA Modules:
  0.0 139.4 jit_solution(6750816232308396523)
XLA Ops:
  0.6 0.0 copy-start.3
  0.6 0.0 copy-start
  1.4 3.6 %count.1 = bf16[16,160,128]{2,1,0:T(8,128)(2,1)} custom-call(s32[1,1]{1,0:T(1,128)S(6)} %copy.12.live_slots, s32[2,88]{1,0:T(2,128)} %bitcast.12, bf16[88,128,128]{2,1,0:T(8,128)(2,1)} %bitcast.7, bf16[128,128]{1,0:T(8,128)(2,1)} %x.1), custom_call_target="tpu_custom_call" | custom-call | flops 2883584 | bytes 3572420 | tf_op jit(solution)/shard_map/count/pallas_call | solution.py:33
  5.0 9.0 %all-to-all-start = ((bf16[16,160,128]{2,1,0:T(8,128)(2,1)}), bf16[16,160,128]{2,1,0:T(8,128)(2,1)}, u32[]{:S(2)}, u32[]{:S(2)}) async-start(bf16[16,160,128]{2,1,0:T(8,128)(2,1)} %count.1), calls=%async_computation | async-start | bytes 1310720 | tf_op jit(solution)/shard_map/all_to_all | solution.py:389
  14.1 0.0 copy-done.3
  14.1 0.0 copy-done
  14.1 2.9 %plan.1 = (f32[16,128]{1,0:T(8,128)S(1)}, s32[1074]{0:T(1024)S(1)}) custom-call(s32[1,1]{1,0:T(1,128)S(6)} %copy.12.live_slots, s32[2,88]{1,0:T(2,128)S(1)} %bitcast.13, bf16[88,128,128]{2,1,0:T(8,128)(2,1)S(1)} %bitcast.8), custom_call_target="tpu_custom_call" | custom-call | flops 23068672 | bytes 2896780 | tf_op jit(solution)/shard_map/plan/pallas_call | solution.py:33
  17.0 0.0 copy-start.1
  17.0 0.0 copy-start.2
  17.0 0.0 copy-start.4
  17.0 14.6 %all-to-all-done.own = bf16[16,160,128]{2,1,0:T(8,128)(2,1)} async-done(((bf16[16,160,128]{2,1,0:T(8,128)(2,1)}), bf16[16,160,128]{2,1,0:T(8,128)(2,1)}, u32[]{:S(2)}, u32[]{:S(2)}) %all-to-all-start) | async-done | bytes 655392 | tf_op jit(solution)/shard_map/all_to_all | solution.py:389
  31.7 1.9 %collective-permute-start = (bf16[16,160,128]{2,1,0:T(8,128)(2,1)}, bf16[16,160,128]{2,1,0:T(8,128)(2,1)S(1)}, u32[]{:S(2)}, u32[]{:S(2)}) collective-permute-start(bf16[16,160,128]{2,1,0:T(8,128)(2,1)} %all-to-all-done.own), channel_id=1, source_target_pairs={{0,16},{16,0},{32,48},{48,32},{64,80},{80,64},{96,112},{112,96},{1... | collective-permute-start | bytes 1966088 | tf_op jit(solution)/shard_map/ppermute | solution.py:402
  33.6 2.3 %collective-permute-done.other = bf16[16,160,128]{2,1,0:T(8,128)(2,1)S(1)} collective-permute-done((bf16[16,160,128]{2,1,0:T(8,128)(2,1)}, bf16[16,160,128]{2,1,0:T(8,128)(2,1)S(1)}, u32[]{:S(2)}, u32[]{:S(2)}) %collective-permute-start) | collective-permute-done | bytes 655392 | tf_op jit(solution)/shard_map/ppermute | solution.py:402
  35.9 3.5 %forward.1 = (bf16[16,136,128]{2,1,0:T(8,128)(2,1)S(1)}, f32[32,128]{1,0:T(8,128)S(1)}) custom-call(s32[1074]{0:T(1024)S(1)} %get-tuple-element.14.plan, bf16[88,128,128]{2,1,0:T(8,128)(2,1)S(1)} %bitcast.9, bf16[16,160,128]{2,1,0:T(8,128)(2,1)} %all-to-all-done.own, bf16[16,160,128]{2,1,0:T(8,128)(2,1)S(1)} %collective-permute-done.other, ...), custom_call_target="tpu_custom_call" | custom-call | flops 369098752 | bytes 4780232 | tf_op jit(solution)/shard_map/forward/pallas_call | solution.py:33
  39.4 32.6 %all_to_all.25.partials = bf16[16,136,128]{2,1,0:T(8,128)(2,1)S(1)} all-to-all(bf16[16,136,128]{2,1,0:T(8,128)(2,1)S(1)} %get-tuple-element.18), channel_id=1, replica_groups=mesh['row'=32,'col'=16] {'col'}, dimensions={0} | all-to-all | bytes 1114112 | tf_op jit(solution)/shard_map/all_to_all | solution.py:419
  72.0 0.0 copy-done.1
  72.0 0.0 copy-done.2
  72.0 0.0 copy-done.4
  72.0 0.9 node.1
  73.0 22.7 %all_to_all.26.message.partials = bf16[16,152,128]{2,1,0:T(8,128)(2,1)S(1)} all-to-all(bf16[16,152,128]{2,1,0:T(8,128)(2,1)S(1)} %get-tuple-element.20), channel_id=1, replica_groups=mesh['row'=32,'col'=16] {'col'}, dimensions={0} | all-to-all | bytes 1245184 | tf_op jit(solution)/shard_map/all_to_all | solution.py:434
  95.7 1.8 %backward_other.1 = bf16[2096,128]{1,0:T(8,128)(2,1)S(1)} custom-call(s32[1074]{0:T(1024)S(1)} %get-tuple-element.14.plan, bf16[88,128,128]{2,1,0:T(8,128)(2,1)S(1)} %bitcast.10, bf16[16,152,128]{2,1,0:T(8,128)(2,1)S(1)} %all_to_all.26.message.partials), custom_call_target="tpu_custom_call" | custom-call | flops 369098752 | bytes 4047048 | tf_op jit(solution)/shard_map/backward_other/pallas_call | solution.py:33
  97.5 1.9 %collective-permute-start.1 = (bf16[2096,128]{1,0:T(8,128)(2,1)S(1)}, bf16[2096,128]{1,0:T(8,128)(2,1)S(1)}, u32[]{:S(2)}, u32[]{:S(2)}) collective-permute-start(bf16[2096,128]{1,0:T(8,128)(2,1)S(1)} %backward_other.1), channel_id=1, source_target_pairs={{0,16},{16,0},{32,48},{48,32},{64,80},{80,64},{96,112},{112,96},{1... | collective-permute-start | bytes 1609736 | tf_op jit(solution)/shard_map/ppermute | solution.py:445
  99.4 1.8 %backward_own.1.own = bf16[16,128,128]{2,1,0:T(8,128)(2,1)S(1)} custom-call(s32[1074]{0:T(1024)S(1)} %get-tuple-element.14.plan, bf16[88,128,128]{2,1,0:T(8,128)(2,1)S(1)} %bitcast.11, bf16[16,152,128]{2,1,0:T(8,128)(2,1)S(1)} %all_to_all.26.message.partials), custom_call_target="tpu_custom_call" | custom-call | flops 369098752 | bytes 4034760 | tf_op jit(solution)/shard_map/backward_own/pallas_call | solution.py:33
  101.2 0.1 collective-permute-done.1.arrived
  101.3 0.2 pair.1
  101.4 25.0 %all_to_all.27.message = bf16[16,152,128]{2,1,0:T(8,128)(2,1)S(1)} all-to-all(bf16[16,152,128]{2,1,0:T(8,128)(2,1)S(1)} %pair.1), channel_id=1, replica_groups={{0,32,64,96,128,160,192,224,256,288,320,352,384,416,448,480},{16,48,80,..., dimensions={0} | all-to-all | bytes 1245184 | tf_op jit(solution)/shard_map/all_to_all | solution.py:462
  126.5 0.7 tail.1
  127.2 4.0 %all-to-all-start.4 = ((f32[16,8,256]{2,1,0:T(8,128)}), f32[16,8,256]{2,1,0:T(8,128)S(1)}, u32[]{:S(2)}, u32[]{:S(2)}) async-start(f32[16,8,256]{2,1,0:T(8,128)} %get-tuple-element.22), calls=%async_computation.4 | async-start | bytes 262144 | tf_op jit(solution)/shard_map/all_to_all | solution.py:470
  131.2 0.8 last.1
  132.0 6.8 %all-to-all-done.4 = f32[16,8,256]{2,1,0:T(8,128)S(1)} async-done(((f32[16,8,256]{2,1,0:T(8,128)}), f32[16,8,256]{2,1,0:T(8,128)S(1)}, u32[]{:S(2)}, u32[]{:S(2)}) %all-to-all-start.4) | async-done | bytes 131104 | tf_op jit(solution)/shard_map/all_to_all | solution.py:470
  138.7 0.7 copy.13
Async XLA Ops:
  0.6 13.4 %copy-start.3 = (s32[1,88,2]{1,2,0:T(2,128)S(1)}, s32[1,88,2]{1,2,0:T(2,128)}, u32[]{:S(2)}) copy-start(s32[1,88,2]{1,2,0:T(2,128)} %param.11) | copy-start | bytes 2116
  0.6 13.4 %copy-start = (bf16[1,88,128,128]{3,2,1,0:T(8,128)(2,1)S(1)}, bf16[1,88,128,128]{3,2,1,0:T(8,128)(2,1)}, u32[]{:S(2)}) copy-start(bf16[1,88,128,128]{3,2,1,0:T(8,128)(2,1)} %param.10) | copy-start | bytes 8650756
  5.0 26.6 %all-to-all-start = ((bf16[16,160,128]{2,1,0:T(8,128)(2,1)}), bf16[16,160,128]{2,1,0:T(8,128)(2,1)}, u32[]{:S(2)}, u32[]{:S(2)}) async-start(bf16[16,160,128]{2,1,0:T(8,128)(2,1)} %count.1), calls=%async_computation | async-start | bytes 1310720 | tf_op jit(solution)/shard_map/all_to_all | solution.py:389
  17.0 55.0 %copy-start.1 = (bf16[128,256]{1,0:T(8,128)(2,1)S(1)}, bf16[128,256]{1,0:T(8,128)(2,1)}, u32[]{:S(2)}) copy-start(bf16[128,256]{1,0:T(8,128)(2,1)} %weight.1) | copy-start | bytes 196612
  17.0 55.0 %copy-start.2 = (bf16[128,256]{1,0:T(8,128)(2,1)S(1)}, bf16[128,256]{1,0:T(8,128)(2,1)}, u32[]{:S(2)}) copy-start(bf16[128,256]{1,0:T(8,128)(2,1)} %cotangent.1) | copy-start | bytes 196612
  17.0 55.0 %copy-start.4 = (f32[256]{0:T(256)S(1)}, f32[256]{0:T(256)}, u32[]{:S(2)}) copy-start(f32[256]{0:T(256)} %param.9) | copy-start | bytes 3076
  31.7 4.2 %collective-permute-start = (bf16[16,160,128]{2,1,0:T(8,128)(2,1)}, bf16[16,160,128]{2,1,0:T(8,128)(2,1)S(1)}, u32[]{:S(2)}, u32[]{:S(2)}) collective-permute-start(bf16[16,160,128]{2,1,0:T(8,128)(2,1)} %all-to-all-done.own), channel_id=1, source_target_pairs={{0,16},{16,0},{32,48},{48,32},{64,80},{80,64},{96,112},{112,96},{1... | collective-permute-start | bytes 1966088 | tf_op jit(solution)/shard_map/ppermute | solution.py:402
  97.5 3.8 %collective-permute-start.1 = (bf16[2096,128]{1,0:T(8,128)(2,1)S(1)}, bf16[2096,128]{1,0:T(8,128)(2,1)S(1)}, u32[]{:S(2)}, u32[]{:S(2)}) collective-permute-start(bf16[2096,128]{1,0:T(8,128)(2,1)S(1)} %backward_other.1), channel_id=1, source_target_pairs={{0,16},{16,0},{32,48},{48,32},{64,80},{80,64},{96,112},{112,96},{1... | collective-permute-start | bytes 1609736 | tf_op jit(solution)/shard_map/ppermute | solution.py:445
  127.2 11.6 %all-to-all-start.4 = ((f32[16,8,256]{2,1,0:T(8,128)}), f32[16,8,256]{2,1,0:T(8,128)S(1)}, u32[]{:S(2)}, u32[]{:S(2)}) async-start(f32[16,8,256]{2,1,0:T(8,128)} %get-tuple-element.22), calls=%async_computation.4 | async-start | bytes 262144 | tf_op jit(solution)/shard_map/all_to_all | solution.py:470

commit v4 on v3

--- a/solution.py
+++ b/solution.py
@@ -72,8 +72,9 @@
     return lax.broadcasted_iota(jnp.int32, (n, n), 0) == lax.broadcasted_iota(jnp.int32, (n, n), 1)
 
 
-def count_kernel(live_slots, coords, tiles, x, message, held, col_acc, arrivals):
-    col_acc[...] = jnp.zeros_like(col_acc)
+def count_kernel(
+    live_slots, coords_in, tiles, x_in, message, held, col_acc, x, coords, arrivals, others
+):
     half = col_acc.shape[0] // 2
     count = live_slots[0, 0]
     parity = lax.axis_index("row") & 1
@@ -84,8 +85,17 @@
         )
         for i in range(PARTS)
     ]
+    place_copy = pltpu.make_async_copy(coords_in, coords, others.at[0])
+    place_copy.start()
     for copy in copies:
         copy.start()
+    x_copy = pltpu.make_async_copy(x_in, x, others.at[1])
+    x_copy.start()
+    col_acc[...] = jnp.zeros_like(col_acc)
+    place_copy.wait()
+    x_copy.wait()
+    for k in range(half):
+        message[k, :BLK] = x[...]
 
     def group(g, carry):
         for u in range(UNROLL):
@@ -105,7 +115,6 @@
     odd = jnp.where(parity == 0, total[half:], total[:half])
     total = jnp.concatenate([even, odd], axis=0).astype(BF16)
     for k in range(half):
-        message[k, :BLK] = x[...]
         message[k, BLK:] = total
 
 
@@ -175,9 +184,7 @@
     scale[...] = factor
     leaving = pltpu.make_async_copy(scale, scale_out, moved.at[1])
     leaving.start()
-    turned = lax.dot_general(
-        eye(BLK).astype(F32), factor, NT, precision=lax.Precision.HIGHEST, preferred_element_type=F32
-    )
+    turned = factor.T
     even, odd = turned[:, :half], turned[:, half:]
     mine = jnp.where(parity == 0, even, odd)
     theirs = jnp.where(parity == 0, odd, even)
@@ -376,12 +383,15 @@
         count_kernel,
         "count",
         (block_counts, coords, tiles, node_inputs),
-        [SMEM, SMEM, ANY, VMEM],
+        [SMEM, ANY, ANY, ANY],
         struct((half, BLK + row_devices, BLK), BF16),
         [
             pltpu.VMEM((slots, BLK, BLK), BF16),
             pltpu.VMEM((row_devices, 16, BLK), F32),
+            pltpu.VMEM((BLK, BLK), BF16),
+            pltpu.SMEM((2, slots), jnp.int32),
             pltpu.SemaphoreType.DMA((PARTS,)),
+            pltpu.SemaphoreType.DMA((2,)),
         ],
         work // 128,
         61,

time: 140 us -> 139 us (level)
  waiting for transfers between devices: 23.8 us -> 17.7 us
  Pallas kernels: 16.1 us -> 21.4 us
    all_to_all x1, waiting for transfers between devices: 14.6 us -> 8.76 us  [per_device(): lax.all_to_all(pieces, 'row', 0, 0, tiled=True, axis_index_groups=parities)]
    pallas_call x9, Pallas kernels: 16.1 us -> 21.4 us  [call(): pl.pallas_call(kernel, out_shape=outs, in_specs=specs, out_specs=out_spec...]
  transfers between devices with their start and end apart: 4 -> 4, of which waited for: 4 -> 4; matrix products, arithmetic and copies ran while one was open for 0% -> 0% of each run, Pallas kernels for 4% -> 7%
where the time goes in v4:
time: 139 us
  blocking collectives  81.5 us (59%)
  Pallas kernels  21.4 us (15%)
  waiting for transfers between devices  17.7 us (13%)
  starting transfers between devices  16.6 us (12%)
  between operations  1.56 us (1%)
    all_to_all x2, blocking collectives, per_device(): message = lax.all_to_all(message, 'col', 0, 0, tiled=True)  56.2 us
    all_to_all x1, blocking collectives, per_device(): lax.all_to_all(message, 'row', 0, 0, tiled=True, axis_index_groups=parities)  25.4 us
    pallas_call x9, Pallas kernels, call(): pl.pallas_call(kernel, out_shape=outs, in_specs=specs, out_specs=out_spec...  21.4 us
    all_to_all x1, starting transfers between devices, per_device(): lax.all_to_all(pieces, 'row', 0, 0, tiled=True, axis_index_groups=parities)  8.82 us
    all_to_all x1, waiting for transfers between devices, per_device(): lax.all_to_all(pieces, 'row', 0, 0, tiled=True, axis_index_groups=parities)  8.76 us
    all_to_all x1, waiting for transfers between devices, per_device(): grad_weight = lax.all_to_all(chunks, 'col', 0, 0, tiled=True)  6.56 us
    all_to_all x1, starting transfers between devices, per_device(): grad_weight = lax.all_to_all(chunks, 'col', 0, 0, tiled=True)  3.94 us
  transfers between devices with their start and end apart: 4, of which 4 were waited for; matrix products, arithmetic and copies ran while one was open for 0% of the time, Pallas kernels for 7%

profile of v4, /device:TPU:8, one launch (start us, length us, event | category | flops | bytes accessed | tf_op | source)
XLA Modules:
  0.0 139.4 jit_solution(4496409745478363092)
XLA Ops:
  0.6 0.0 copy-start.3
  0.6 0.0 copy-start
  1.4 3.6 %count.1 = bf16[16,160,128]{2,1,0:T(8,128)(2,1)} custom-call(s32[1,1]{1,0:T(1,128)S(6)} %copy.12.live_slots, s32[2,88]{1,0:T(2,128)} %bitcast.12, bf16[88,128,128]{2,1,0:T(8,128)(2,1)} %bitcast.7, bf16[128,128]{1,0:T(8,128)(2,1)} %x_in.1), custom_call_target="tpu_custom_call" | custom-call | flops 2883584 | bytes 3572420 | tf_op jit(solution)/shard_map/count/pallas_call | solution.py:33
  5.0 8.8 %all-to-all-start = ((bf16[16,160,128]{2,1,0:T(8,128)(2,1)}), bf16[16,160,128]{2,1,0:T(8,128)(2,1)}, u32[]{:S(2)}, u32[]{:S(2)}) async-start(bf16[16,160,128]{2,1,0:T(8,128)(2,1)} %count.1), calls=%async_computation | async-start | bytes 1310720 | tf_op jit(solution)/shard_map/all_to_all | solution.py:399
  13.9 0.0 copy-done.3
  13.9 0.0 copy-done
  13.9 7.7 %plan.1 = (f32[16,128]{1,0:T(8,128)S(1)}, s32[1074]{0:T(1024)S(1)}) custom-call(s32[1,1]{1,0:T(1,128)S(6)} %copy.12.live_slots, s32[2,88]{1,0:T(2,128)S(1)} %bitcast.13, bf16[88,128,128]{2,1,0:T(8,128)(2,1)S(1)} %bitcast.8), custom_call_target="tpu_custom_call" | custom-call | flops 23068672 | bytes 2896780 | tf_op jit(solution)/shard_map/plan/pallas_call | solution.py:33
  21.6 0.0 copy-start.1
  21.6 0.0 copy-start.2
  21.6 0.0 copy-start.4
  21.6 8.8 %all-to-all-done.own = bf16[16,160,128]{2,1,0:T(8,128)(2,1)} async-done(((bf16[16,160,128]{2,1,0:T(8,128)(2,1)}), bf16[16,160,128]{2,1,0:T(8,128)(2,1)}, u32[]{:S(2)}, u32[]{:S(2)}) %all-to-all-start) | async-done | bytes 655392 | tf_op jit(solution)/shard_map/all_to_all | solution.py:399
  30.4 1.9 %collective-permute-start = (bf16[16,160,128]{2,1,0:T(8,128)(2,1)}, bf16[16,160,128]{2,1,0:T(8,128)(2,1)S(1)}, u32[]{:S(2)}, u32[]{:S(2)}) collective-permute-start(bf16[16,160,128]{2,1,0:T(8,128)(2,1)} %all-to-all-done.own), channel_id=1, source_target_pairs={{0,16},{16,0},{32,48},{48,32},{64,80},{80,64},{96,112},{112,96},{1... | collective-permute-start | bytes 1966088 | tf_op jit(solution)/shard_map/ppermute | solution.py:412
  32.3 2.3 %collective-permute-done.other = bf16[16,160,128]{2,1,0:T(8,128)(2,1)S(1)} collective-permute-done((bf16[16,160,128]{2,1,0:T(8,128)(2,1)}, bf16[16,160,128]{2,1,0:T(8,128)(2,1)S(1)}, u32[]{:S(2)}, u32[]{:S(2)}) %collective-permute-start) | collective-permute-done | bytes 655392 | tf_op jit(solution)/shard_map/ppermute | solution.py:412
  34.6 4.0 %forward.1 = (bf16[16,136,128]{2,1,0:T(8,128)(2,1)S(1)}, f32[32,128]{1,0:T(8,128)S(1)}) custom-call(s32[1074]{0:T(1024)S(1)} %get-tuple-element.14.plan, bf16[88,128,128]{2,1,0:T(8,128)(2,1)S(1)} %bitcast.9, bf16[16,160,128]{2,1,0:T(8,128)(2,1)} %all-to-all-done.own, bf16[16,160,128]{2,1,0:T(8,128)(2,1)S(1)} %collective-permute-done.other, ...), custom_call_target="tpu_custom_call" | custom-call | flops 369098752 | bytes 4780232 | tf_op jit(solution)/shard_map/forward/pallas_call | solution.py:33
  38.6 33.7 %all_to_all.25.partials = bf16[16,136,128]{2,1,0:T(8,128)(2,1)S(1)} all-to-all(bf16[16,136,128]{2,1,0:T(8,128)(2,1)S(1)} %get-tuple-element.18), channel_id=1, replica_groups=mesh['row'=32,'col'=16] {'col'}, dimensions={0} | all-to-all | bytes 1114112 | tf_op jit(solution)/shard_map/all_to_all | solution.py:429
  72.3 0.0 copy-done.1
  72.3 0.0 copy-done.2
  72.3 0.0 copy-done.4
  72.3 0.9 node.1
  73.2 22.5 %all_to_all.26.message.partials = bf16[16,152,128]{2,1,0:T(8,128)(2,1)S(1)} all-to-all(bf16[16,152,128]{2,1,0:T(8,128)(2,1)S(1)} %get-tuple-element.20), channel_id=1, replica_groups=mesh['row'=32,'col'=16] {'col'}, dimensions={0} | all-to-all | bytes 1245184 | tf_op jit(solution)/shard_map/all_to_all | solution.py:444
  95.7 1.8 %backward_other.1 = bf16[2096,128]{1,0:T(8,128)(2,1)S(1)} custom-call(s32[1074]{0:T(1024)S(1)} %get-tuple-element.14.plan, bf16[88,128,128]{2,1,0:T(8,128)(2,1)S(1)} %bitcast.10, bf16[16,152,128]{2,1,0:T(8,128)(2,1)S(1)} %all_to_all.26.message.partials), custom_call_target="tpu_custom_call" | custom-call | flops 369098752 | bytes 4047048 | tf_op jit(solution)/shard_map/backward_other/pallas_call | solution.py:33
  97.5 1.9 %collective-permute-start.1 = (bf16[2096,128]{1,0:T(8,128)(2,1)S(1)}, bf16[2096,128]{1,0:T(8,128)(2,1)S(1)}, u32[]{:S(2)}, u32[]{:S(2)}) collective-permute-start(bf16[2096,128]{1,0:T(8,128)(2,1)S(1)} %backward_other.1), channel_id=1, source_target_pairs={{0,16},{16,0},{32,48},{48,32},{64,80},{80,64},{96,112},{112,96},{1... | collective-permute-start | bytes 1609736 | tf_op jit(solution)/shard_map/ppermute | solution.py:455
  99.4 1.8 %backward_own.1.own = bf16[16,128,128]{2,1,0:T(8,128)(2,1)S(1)} custom-call(s32[1074]{0:T(1024)S(1)} %get-tuple-element.14.plan, bf16[88,128,128]{2,1,0:T(8,128)(2,1)S(1)} %bitcast.11, bf16[16,152,128]{2,1,0:T(8,128)(2,1)S(1)} %all_to_all.26.message.partials), custom_call_target="tpu_custom_call" | custom-call | flops 369098752 | bytes 4034760 | tf_op jit(solution)/shard_map/backward_own/pallas_call | solution.py:33
  101.2 0.1 collective-permute-done.1.arrived
  101.3 0.2 pair.1
  101.5 25.4 %all_to_all.27.message = bf16[16,152,128]{2,1,0:T(8,128)(2,1)S(1)} all-to-all(bf16[16,152,128]{2,1,0:T(8,128)(2,1)S(1)} %pair.1), channel_id=1, replica_groups={{0,32,64,96,128,160,192,224,256,288,320,352,384,416,448,480},{16,48,80,..., dimensions={0} | all-to-all | bytes 1245184 | tf_op jit(solution)/shard_map/all_to_all | solution.py:472
  126.8 0.7 tail.1
  127.5 3.9 %all-to-all-start.4 = ((f32[16,8,256]{2,1,0:T(8,128)}), f32[16,8,256]{2,1,0:T(8,128)S(1)}, u32[]{:S(2)}, u32[]{:S(2)}) async-start(f32[16,8,256]{2,1,0:T(8,128)} %get-tuple-element.22), calls=%async_computation.4 | async-start | bytes 262144 | tf_op jit(solution)/shard_map/all_to_all | solution.py:480
  131.5 0.8 last.1
  132.2 6.6 %all-to-all-done.4 = f32[16,8,256]{2,1,0:T(8,128)S(1)} async-done(((f32[16,8,256]{2,1,0:T(8,128)}), f32[16,8,256]{2,1,0:T(8,128)S(1)}, u32[]{:S(2)}, u32[]{:S(2)}) %all-to-all-start.4) | async-done | bytes 131104 | tf_op jit(solution)/shard_map/all_to_all | solution.py:480
  138.8 0.7 copy.13
Async XLA Ops:
  0.6 13.2 %copy-start.3 = (s32[1,88,2]{1,2,0:T(2,128)S(1)}, s32[1,88,2]{1,2,0:T(2,128)}, u32[]{:S(2)}) copy-start(s32[1,88,2]{1,2,0:T(2,128)} %param.11) | copy-start | bytes 2116
  0.6 13.2 %copy-start = (bf16[1,88,128,128]{3,2,1,0:T(8,128)(2,1)S(1)}, bf16[1,88,128,128]{3,2,1,0:T(8,128)(2,1)}, u32[]{:S(2)}) copy-start(bf16[1,88,128,128]{3,2,1,0:T(8,128)(2,1)} %param.10) | copy-start | bytes 8650756
  5.0 25.4 %all-to-all-start = ((bf16[16,160,128]{2,1,0:T(8,128)(2,1)}), bf16[16,160,128]{2,1,0:T(8,128)(2,1)}, u32[]{:S(2)}, u32[]{:S(2)}) async-start(bf16[16,160,128]{2,1,0:T(8,128)(2,1)} %count.1), calls=%async_computation | async-start | bytes 1310720 | tf_op jit(solution)/shard_map/all_to_all | solution.py:399
  21.6 50.7 %copy-start.1 = (bf16[128,256]{1,0:T(8,128)(2,1)S(1)}, bf16[128,256]{1,0:T(8,128)(2,1)}, u32[]{:S(2)}) copy-start(bf16[128,256]{1,0:T(8,128)(2,1)} %weight.1) | copy-start | bytes 196612
  21.6 50.6 %copy-start.2 = (bf16[128,256]{1,0:T(8,128)(2,1)S(1)}, bf16[128,256]{1,0:T(8,128)(2,1)}, u32[]{:S(2)}) copy-start(bf16[128,256]{1,0:T(8,128)(2,1)} %cotangent.1) | copy-start | bytes 196612
  21.6 50.6 %copy-start.4 = (f32[256]{0:T(256)S(1)}, f32[256]{0:T(256)}, u32[]{:S(2)}) copy-start(f32[256]{0:T(256)} %param.9) | copy-start | bytes 3076
  30.4 4.2 %collective-permute-start = (bf16[16,160,128]{2,1,0:T(8,128)(2,1)}, bf16[16,160,128]{2,1,0:T(8,128)(2,1)S(1)}, u32[]{:S(2)}, u32[]{:S(2)}) collective-permute-start(bf16[16,160,128]{2,1,0:T(8,128)(2,1)} %all-to-all-done.own), channel_id=1, source_target_pairs={{0,16},{16,0},{32,48},{48,32},{64,80},{80,64},{96,112},{112,96},{1... | collective-permute-start | bytes 1966088 | tf_op jit(solution)/shard_map/ppermute | solution.py:412
  97.5 3.8 %collective-permute-start.1 = (bf16[2096,128]{1,0:T(8,128)(2,1)S(1)}, bf16[2096,128]{1,0:T(8,128)(2,1)S(1)}, u32[]{:S(2)}, u32[]{:S(2)}) collective-permute-start(bf16[2096,128]{1,0:T(8,128)(2,1)S(1)} %backward_other.1), channel_id=1, source_target_pairs={{0,16},{16,0},{32,48},{48,32},{64,80},{80,64},{96,112},{112,96},{1... | collective-permute-start | bytes 1609736 | tf_op jit(solution)/shard_map/ppermute | solution.py:455
  127.5 11.3 %all-to-all-start.4 = ((f32[16,8,256]{2,1,0:T(8,128)}), f32[16,8,256]{2,1,0:T(8,128)S(1)}, u32[]{:S(2)}, u32[]{:S(2)}) async-start(f32[16,8,256]{2,1,0:T(8,128)} %get-tuple-element.22), calls=%async_computation.4 | async-start | bytes 262144 | tf_op jit(solution)/shard_map/all_to_all | solution.py:480

commit v5 on v4

--- a/solution.py
+++ b/solution.py
@@ -209,6 +209,7 @@
         for j in range(fixed):
             total += pair(p, j)
         acc[p] = total
+        message[p, :BLK] = total.astype(BF16)
 
     @pl.when(plan[lengths + row_blocks + row_devices] > 2 * fixed)
     def _():
@@ -219,11 +220,11 @@
                 return carry
 
             lax.fori_loop(fixed, (plan[lengths + p] + 1) // 2, more, 0)
+            message[p, :BLK] = acc[p].astype(BF16)
 
     arriving.wait()
     line = lax.broadcasted_iota(jnp.int32, (TAIL, BLK), 0)
     for p in range(row_blocks):
-        message[p, :BLK] = acc[p].astype(BF16)
         high, low = whole_parts(rows[p : p + 1])
         extra = jnp.where(line == 0, high, jnp.where(line == 1, low, 0.0))
         message[p, BLK:] = extra.astype(BF16)

time: 139 us -> 140 us (level)
  waiting for transfers between devices: 17.7 us -> 23.3 us
  Pallas kernels: 21.4 us -> 16 us
    all_to_all x1, waiting for transfers between devices: 8.76 us -> 14.3 us  [per_device(): lax.all_to_all(pieces, 'row', 0, 0, tiled=True, axis_index_groups=parities)]
    pallas_call x9, Pallas kernels: 21.4 us -> 16 us  [call(): pl.pallas_call(kernel, out_shape=outs, in_specs=specs, out_specs=out_spec...]
  transfers between devices with their start and end apart: 4 -> 4, of which waited for: 4 -> 4; matrix products, arithmetic and copies ran while one was open for 0% -> 0% of each run, Pallas kernels for 7% -> 4%
where the time goes in v5:
time: 140 us; the launch traced here: 139 us
  blocking collectives  81.4 us (58%)
  waiting for transfers between devices  23.3 us (17%)
  starting transfers between devices  16.6 us (12%)
  Pallas kernels  16 us (11%)
  between operations  1.56 us (1%)
    all_to_all x2, blocking collectives, per_device(): message = lax.all_to_all(message, 'col', 0, 0, tiled=True)  56.3 us
    all_to_all x1, blocking collectives, per_device(): lax.all_to_all(message, 'row', 0, 0, tiled=True, axis_index_groups=parities)  25 us
    pallas_call x9, Pallas kernels, call(): pl.pallas_call(kernel, out_shape=outs, in_specs=specs, out_specs=out_spec...  16 us
    all_to_all x1, waiting for transfers between devices, per_device(): lax.all_to_all(pieces, 'row', 0, 0, tiled=True, axis_index_groups=parities)  14.3 us
    all_to_all x1, starting transfers between devices, per_device(): lax.all_to_all(pieces, 'row', 0, 0, tiled=True, axis_index_groups=parities)  8.73 us
    all_to_all x1, waiting for transfers between devices, per_device(): grad_weight = lax.all_to_all(chunks, 'col', 0, 0, tiled=True)  6.57 us
    all_to_all x1, starting transfers between devices, per_device(): grad_weight = lax.all_to_all(chunks, 'col', 0, 0, tiled=True)  4.09 us
  transfers between devices with their start and end apart: 4, of which 4 were waited for; matrix products, arithmetic and copies ran while one was open for 0% of the time, Pallas kernels for 4%

profile of v5, /device:TPU:8, one launch (start us, length us, event | category | flops | bytes accessed | tf_op | source)
XLA Modules:
  0.0 139.5 jit_solution(3699684145179422242)
XLA Ops:
  0.6 0.0 copy-start.3
  0.6 0.0 copy-start
  1.4 3.0 %count.1 = bf16[16,160,128]{2,1,0:T(8,128)(2,1)} custom-call(s32[1,1]{1,0:T(1,128)S(6)} %copy.12.live_slots, s32[2,88]{1,0:T(2,128)} %bitcast.12, bf16[88,128,128]{2,1,0:T(8,128)(2,1)} %bitcast.7, bf16[128,128]{1,0:T(8,128)(2,1)} %x_in.1), custom_call_target="tpu_custom_call" | custom-call | flops 2883584 | bytes 3572420 | tf_op jit(solution)/shard_map/count/pallas_call | solution.py:33
  4.4 8.7 %all-to-all-start = ((bf16[16,160,128]{2,1,0:T(8,128)(2,1)}), bf16[16,160,128]{2,1,0:T(8,128)(2,1)}, u32[]{:S(2)}, u32[]{:S(2)}) async-start(bf16[16,160,128]{2,1,0:T(8,128)(2,1)} %count.1), calls=%async_computation | async-start | bytes 1310720 | tf_op jit(solution)/shard_map/all_to_all | solution.py:400
  13.2 0.0 copy-done.3
  13.2 0.0 copy-done
  13.2 3.6 %plan.1 = (f32[16,128]{1,0:T(8,128)S(1)}, s32[1074]{0:T(1024)S(1)}) custom-call(s32[1,1]{1,0:T(1,128)S(6)} %copy.12.live_slots, s32[2,88]{1,0:T(2,128)S(1)} %bitcast.13, bf16[88,128,128]{2,1,0:T(8,128)(2,1)S(1)} %bitcast.8), custom_call_target="tpu_custom_call" | custom-call | flops 23068672 | bytes 2896780 | tf_op jit(solution)/shard_map/plan/pallas_call | solution.py:33
  16.8 0.0 copy-start.1
  16.8 0.0 copy-start.2
  16.8 0.0 copy-start.4
  16.9 14.3 %all-to-all-done.own = bf16[16,160,128]{2,1,0:T(8,128)(2,1)} async-done(((bf16[16,160,128]{2,1,0:T(8,128)(2,1)}), bf16[16,160,128]{2,1,0:T(8,128)(2,1)}, u32[]{:S(2)}, u32[]{:S(2)}) %all-to-all-start) | async-done | bytes 655392 | tf_op jit(solution)/shard_map/all_to_all | solution.py:400
  31.2 1.9 %collective-permute-start = (bf16[16,160,128]{2,1,0:T(8,128)(2,1)}, bf16[16,160,128]{2,1,0:T(8,128)(2,1)S(1)}, u32[]{:S(2)}, u32[]{:S(2)}) collective-permute-start(bf16[16,160,128]{2,1,0:T(8,128)(2,1)} %all-to-all-done.own), channel_id=1, source_target_pairs={{0,16},{16,0},{32,48},{48,32},{64,80},{80,64},{96,112},{112,96},{1... | collective-permute-start | bytes 1966088 | tf_op jit(solution)/shard_map/ppermute | solution.py:413
  33.1 2.3 %collective-permute-done.other = bf16[16,160,128]{2,1,0:T(8,128)(2,1)S(1)} collective-permute-done((bf16[16,160,128]{2,1,0:T(8,128)(2,1)}, bf16[16,160,128]{2,1,0:T(8,128)(2,1)S(1)}, u32[]{:S(2)}, u32[]{:S(2)}) %collective-permute-start) | collective-permute-done | bytes 655392 | tf_op jit(solution)/shard_map/ppermute | solution.py:413
  35.3 3.3 %forward.1 = (bf16[16,136,128]{2,1,0:T(8,128)(2,1)S(1)}, f32[32,128]{1,0:T(8,128)S(1)}) custom-call(s32[1074]{0:T(1024)S(1)} %get-tuple-element.14.plan, bf16[88,128,128]{2,1,0:T(8,128)(2,1)S(1)} %bitcast.9, bf16[16,160,128]{2,1,0:T(8,128)(2,1)} %all-to-all-done.own, bf16[16,160,128]{2,1,0:T(8,128)(2,1)S(1)} %collective-permute-done.other, ...), custom_call_target="tpu_custom_call" | custom-call | flops 369098752 | bytes 4780232 | tf_op jit(solution)/shard_map/forward/pallas_call | solution.py:33
  38.7 33.8 %all_to_all.25.partials = bf16[16,136,128]{2,1,0:T(8,128)(2,1)S(1)} all-to-all(bf16[16,136,128]{2,1,0:T(8,128)(2,1)S(1)} %get-tuple-element.18), channel_id=1, replica_groups=mesh['row'=32,'col'=16] {'col'}, dimensions={0} | all-to-all | bytes 1114112 | tf_op jit(solution)/shard_map/all_to_all | solution.py:430
  72.5 0.0 copy-done.1
  72.5 0.0 copy-done.2
  72.5 0.0 copy-done.4
  72.5 0.9 node.1
  73.4 22.5 %all_to_all.26.message.partials = bf16[16,152,128]{2,1,0:T(8,128)(2,1)S(1)} all-to-all(bf16[16,152,128]{2,1,0:T(8,128)(2,1)S(1)} %get-tuple-element.20), channel_id=1, replica_groups=mesh['row'=32,'col'=16] {'col'}, dimensions={0} | all-to-all | bytes 1245184 | tf_op jit(solution)/shard_map/all_to_all | solution.py:445
  95.9 1.8 %backward_other.1 = bf16[2096,128]{1,0:T(8,128)(2,1)S(1)} custom-call(s32[1074]{0:T(1024)S(1)} %get-tuple-element.14.plan, bf16[88,128,128]{2,1,0:T(8,128)(2,1)S(1)} %bitcast.10, bf16[16,152,128]{2,1,0:T(8,128)(2,1)S(1)} %all_to_all.26.message.partials), custom_call_target="tpu_custom_call" | custom-call | flops 369098752 | bytes 4047048 | tf_op jit(solution)/shard_map/backward_other/pallas_call | solution.py:33
  97.7 1.9 %collective-permute-start.1 = (bf16[2096,128]{1,0:T(8,128)(2,1)S(1)}, bf16[2096,128]{1,0:T(8,128)(2,1)S(1)}, u32[]{:S(2)}, u32[]{:S(2)}) collective-permute-start(bf16[2096,128]{1,0:T(8,128)(2,1)S(1)} %backward_other.1), channel_id=1, source_target_pairs={{0,16},{16,0},{32,48},{48,32},{64,80},{80,64},{96,112},{112,96},{1... | collective-permute-start | bytes 1609736 | tf_op jit(solution)/shard_map/ppermute | solution.py:456
  99.6 1.8 %backward_own.1.own = bf16[16,128,128]{2,1,0:T(8,128)(2,1)S(1)} custom-call(s32[1074]{0:T(1024)S(1)} %get-tuple-element.14.plan, bf16[88,128,128]{2,1,0:T(8,128)(2,1)S(1)} %bitcast.11, bf16[16,152,128]{2,1,0:T(8,128)(2,1)S(1)} %all_to_all.26.message.partials), custom_call_target="tpu_custom_call" | custom-call | flops 369098752 | bytes 4034760 | tf_op jit(solution)/shard_map/backward_own/pallas_call | solution.py:33
  101.4 0.1 collective-permute-done.1.arrived
  101.5 0.2 pair.1
  101.7 25.0 %all_to_all.27.message = bf16[16,152,128]{2,1,0:T(8,128)(2,1)S(1)} all-to-all(bf16[16,152,128]{2,1,0:T(8,128)(2,1)S(1)} %pair.1), channel_id=1, replica_groups={{0,32,64,96,128,160,192,224,256,288,320,352,384,416,448,480},{16,48,80,..., dimensions={0} | all-to-all | bytes 1245184 | tf_op jit(solution)/shard_map/all_to_all | solution.py:473
  126.7 0.7 tail.1
  127.4 4.1 %all-to-all-start.4 = ((f32[16,8,256]{2,1,0:T(8,128)}), f32[16,8,256]{2,1,0:T(8,128)S(1)}, u32[]{:S(2)}, u32[]{:S(2)}) async-start(f32[16,8,256]{2,1,0:T(8,128)} %get-tuple-element.22), calls=%async_computation.4 | async-start | bytes 262144 | tf_op jit(solution)/shard_map/all_to_all | solution.py:481
  131.5 0.8 last.1
  132.3 6.6 %all-to-all-done.4 = f32[16,8,256]{2,1,0:T(8,128)S(1)} async-done(((f32[16,8,256]{2,1,0:T(8,128)}), f32[16,8,256]{2,1,0:T(8,128)S(1)}, u32[]{:S(2)}, u32[]{:S(2)}) %all-to-all-start.4) | async-done | bytes 131104 | tf_op jit(solution)/shard_map/all_to_all | solution.py:481
  138.8 0.7 copy.13
Async XLA Ops:
  0.6 12.5 %copy-start.3 = (s32[1,88,2]{1,2,0:T(2,128)S(1)}, s32[1,88,2]{1,2,0:T(2,128)}, u32[]{:S(2)}) copy-start(s32[1,88,2]{1,2,0:T(2,128)} %param.11) | copy-start | bytes 2116
  0.6 12.5 %copy-start = (bf16[1,88,128,128]{3,2,1,0:T(8,128)(2,1)S(1)}, bf16[1,88,128,128]{3,2,1,0:T(8,128)(2,1)}, u32[]{:S(2)}) copy-start(bf16[1,88,128,128]{3,2,1,0:T(8,128)(2,1)} %param.10) | copy-start | bytes 8650756
  4.4 26.7 %all-to-all-start = ((bf16[16,160,128]{2,1,0:T(8,128)(2,1)}), bf16[16,160,128]{2,1,0:T(8,128)(2,1)}, u32[]{:S(2)}, u32[]{:S(2)}) async-start(bf16[16,160,128]{2,1,0:T(8,128)(2,1)} %count.1), calls=%async_computation | async-start | bytes 1310720 | tf_op jit(solution)/shard_map/all_to_all | solution.py:400
  16.8 55.7 %copy-start.1 = (bf16[128,256]{1,0:T(8,128)(2,1)S(1)}, bf16[128,256]{1,0:T(8,128)(2,1)}, u32[]{:S(2)}) copy-start(bf16[128,256]{1,0:T(8,128)(2,1)} %weight.1) | copy-start | bytes 196612
  16.8 55.7 %copy-start.2 = (bf16[128,256]{1,0:T(8,128)(2,1)S(1)}, bf16[128,256]{1,0:T(8,128)(2,1)}, u32[]{:S(2)}) copy-start(bf16[128,256]{1,0:T(8,128)(2,1)} %cotangent.1) | copy-start | bytes 196612
  16.8 55.7 %copy-start.4 = (f32[256]{0:T(256)S(1)}, f32[256]{0:T(256)}, u32[]{:S(2)}) copy-start(f32[256]{0:T(256)} %param.9) | copy-start | bytes 3076
  31.2 4.2 %collective-permute-start = (bf16[16,160,128]{2,1,0:T(8,128)(2,1)}, bf16[16,160,128]{2,1,0:T(8,128)(2,1)S(1)}, u32[]{:S(2)}, u32[]{:S(2)}) collective-permute-start(bf16[16,160,128]{2,1,0:T(8,128)(2,1)} %all-to-all-done.own), channel_id=1, source_target_pairs={{0,16},{16,0},{32,48},{48,32},{64,80},{80,64},{96,112},{112,96},{1... | collective-permute-start | bytes 1966088 | tf_op jit(solution)/shard_map/ppermute | solution.py:413
  97.7 3.8 %collective-permute-start.1 = (bf16[2096,128]{1,0:T(8,128)(2,1)S(1)}, bf16[2096,128]{1,0:T(8,128)(2,1)S(1)}, u32[]{:S(2)}, u32[]{:S(2)}) collective-permute-start(bf16[2096,128]{1,0:T(8,128)(2,1)S(1)} %backward_other.1), channel_id=1, source_target_pairs={{0,16},{16,0},{32,48},{48,32},{64,80},{80,64},{96,112},{112,96},{1... | collective-permute-start | bytes 1609736 | tf_op jit(solution)/shard_map/ppermute | solution.py:456
  127.4 11.4 %all-to-all-start.4 = ((f32[16,8,256]{2,1,0:T(8,128)}), f32[16,8,256]{2,1,0:T(8,128)S(1)}, u32[]{:S(2)}, u32[]{:S(2)}) async-start(f32[16,8,256]{2,1,0:T(8,128)} %get-tuple-element.22), calls=%async_computation.4 | async-start | bytes 262144 | tf_op jit(solution)/shard_map/all_to_all | solution.py:481
